TPU v7x, 128 devices: a whole 4x4x4 slice. The times are simulated.
128 devices in a mesh: dp: 8 (over x, z_hi), row: 16 (over y, z_lo, core).
Axes of the slice: x: 4, y: 4, z: 4 (z_hi: 2, z_lo: 2; z = z_hi * 2 + z_lo), core: 2. Of those that a mesh axis runs over, the one named last changes fastest.
Arguments:
- pair_rep: bfloat16 [8, 384, 384, 128], P('dp', 'row'), may hold values from -6 to 6
- grad_out: bfloat16 [8, 384, 384, 128], P('dp', 'row'), may hold values from -6 to 6
- crop_len: int32 [8], P('dp'), may hold values from 288 to 384, as said below
- ln_gain: float32 [128], replicated, may hold values from 0.25 to 1.75
- ln_bias: float32 [128], replicated, may hold values from -3 to 3
- w_proj: bfloat16 [128, 512], replicated, may hold values from -0.5 to 0.5
- gate_bias: float32 [128], replicated, may hold values from -4 to 4
- w_bias: bfloat16 [128, 4], replicated, may hold values from -0.5 to 0.5
- w_out: bfloat16 [128, 128], replicated, may hold values from -0.5 to 0.5
Outputs:
- pair_grad: bfloat16 [8, 384, 384, 128], P('dp', 'row')
- proj_grad: float32 [128, 512], replicated
- gate_bias_grad: float32 [128], replicated
- bias_w_grad: float32 [128, 4], replicated
- out_w_grad: float32 [128, 128], replicated
- gain_grad: float32 [128], replicated
- shift_grad: float32 [128], replicated
Inputs may be any that keep to these rules, and one draw needn't show every extreme that they name: `crop_len`: every crop is padded to 384; in every draw one crop fills all 384 residues and one has 288.
All inputs are finite; a program needn't handle non-finite values.
Results may differ from a plain program's by a relative error of at most 0.025.
Values may be sent and summed in bfloat16 or wider, within the bound.
No kernel may reach another device: no remote copies, remote signals or barrier semaphores. Data moves between devices by JAX's collectives and lax.ppermute only.
A program may use at most 128 MiB of HBM per device.

v0:
```python
import math

import jax
import jax.numpy as jnp
from jax import lax
from jax.sharding import PartitionSpec as P

EPSILON = 1e-05


def layer_norm(values_in, scale_vec, shift_vec):
    center = jnp.mean(values_in, axis=-1, keepdims=True)
    spread = jnp.mean(jnp.square(values_in - center), axis=-1, keepdims=True)
    return (values_in - center) * lax.rsqrt(spread + EPSILON) * scale_vec + shift_vec


def body(pair_rep, grad_out, crop_len, ln_gain, ln_bias, w_proj, gate_bias, w_bias, w_out):
    pair_local = pair_rep[0]
    cot_local = grad_out[0]
    length = crop_len[0]
    row_count, crop_size, channels = pair_local.shape
    num_heads = w_bias.shape[1]
    head_size = channels // num_heads
    my_index = lax.axis_index("row")
    positions = jnp.arange(crop_size, dtype=jnp.int32)
    in_crop = positions < length
    own_rows = my_index * row_count + jnp.arange(row_count, dtype=jnp.int32)
    row_live = own_rows < length
    cot_masked = jnp.where(
        row_live[:, None, None] & in_crop[None, :, None], cot_local, jnp.zeros_like(cot_local)
    )
    cols_pair, cols_cot = (
        lax.all_to_all(pair_local, "row", split_axis=1, concat_axis=0, tiled=True),
        lax.all_to_all(cot_masked, "row", split_axis=1, concat_axis=0, tiled=True),
    )
    cols_f = cols_pair.astype(jnp.float32)
    normed_f, side_back = jax.vjp(layer_norm, pair_local.astype(jnp.float32), ln_gain, ln_bias)
    normed = normed_f.astype(jnp.bfloat16)
    logits = jnp.dot(normed.reshape(-1, channels), w_bias, preferred_element_type=jnp.float32)
    logits = logits.astype(jnp.bfloat16).reshape(row_count, crop_size, num_heads).transpose(2, 0, 1)
    bias_plane = lax.all_gather(logits, "row", axis=1, tiled=True)
    block_width = 4
    block_count = row_count // block_width
    head_shape = (crop_size, block_width, num_heads, head_size)
    root_size = math.sqrt(head_size)

    def block_step(block_index, carry):
        dn_cols, bias_grad, proj_grad, gate_grad, out_grad = carry
        offset = block_index * block_width
        pair_blk = lax.dynamic_slice_in_dim(cols_f, offset, block_width, 1)
        cot_blk = lax.dynamic_slice_in_dim(cols_cot, offset, block_width, 1)
        normed_blk = layer_norm(pair_blk, ln_gain, ln_bias)
        flat_blk = normed_blk.astype(jnp.bfloat16).reshape(-1, channels)
        projected = jnp.dot(flat_blk, w_proj, preferred_element_type=jnp.float32).reshape(
            crop_size, block_width, 4 * channels
        )
        query_blk = (projected[..., :channels] / root_size).astype(jnp.bfloat16).reshape(head_shape)
        key_blk = projected[..., channels : 2 * channels].astype(jnp.bfloat16).reshape(head_shape)
        value_blk = (
            projected[..., 2 * channels : 3 * channels].astype(jnp.bfloat16).reshape(head_shape)
        )
        gate_blk = jax.nn.sigmoid(projected[..., 3 * channels :] + gate_bias).reshape(head_shape)
        scores = (
            jnp.einsum("ibhd,kbhd->bhki", query_blk, key_blk, preferred_element_type=jnp.float32)
            + bias_plane[None]
        )
        exponent = jnp.where(in_crop[None, None, :, None], jnp.exp(scores), 0.0)
        weights = exponent / jnp.sum(exponent, axis=2, keepdims=True)
        weights_b = weights.astype(jnp.bfloat16)
        attended = jnp.einsum(
            "bhki,kbhd->ibhd", weights_b, value_blk, preferred_element_type=jnp.float32
        )
        output_blk = (gate_blk * attended).astype(jnp.bfloat16).reshape(-1, channels)
        flat_cot = cot_blk.reshape(-1, channels)
        d_out = jnp.dot(flat_cot, w_out.T, preferred_element_type=jnp.float32).reshape(head_shape)
        d_gate = d_out * attended * gate_blk * (1.0 - gate_blk)
        d_attended = (d_out * gate_blk).astype(jnp.bfloat16)
        d_weights = jnp.einsum(
            "ibhd,kbhd->bhki", d_attended, value_blk, preferred_element_type=jnp.float32
        )
        d_values = jnp.einsum(
            "bhki,ibhd->kbhd", weights_b, d_attended, preferred_element_type=jnp.float32
        )
        d_scores = weights * (d_weights - jnp.sum(weights * d_weights, axis=2, keepdims=True))
        d_scores_b = d_scores.astype(jnp.bfloat16)
        d_query = (
            jnp.einsum("bhki,kbhd->ibhd", d_scores_b, key_blk, preferred_element_type=jnp.float32)
            / root_size
        )
        d_keys = jnp.einsum(
            "bhki,ibhd->kbhd", d_scores_b, query_blk, preferred_element_type=jnp.float32
        )
        pieces = [
            piece_grad.reshape(crop_size, block_width, channels)
            for piece_grad in (d_query, d_keys, d_values, d_gate)
        ]
        d_proj = jnp.concatenate(pieces, axis=-1).astype(jnp.bfloat16).reshape(-1, 4 * channels)
        d_normed = jnp.dot(d_proj, w_proj.T, preferred_element_type=jnp.float32).reshape(
            crop_size, block_width, channels
        )
        dn_cols = lax.dynamic_update_slice_in_dim(dn_cols, d_normed, offset, 1)
        bias_grad = bias_grad + jnp.sum(d_scores, axis=0)
        proj_grad = proj_grad + jnp.dot(flat_blk.T, d_proj, preferred_element_type=jnp.float32)
        gate_grad = gate_grad + jnp.sum(d_gate.reshape(-1, channels), axis=0)
        out_grad = out_grad + jnp.dot(output_blk.T, flat_cot, preferred_element_type=jnp.float32)
        return (dn_cols, bias_grad, proj_grad, gate_grad, out_grad)

    init = (
        jnp.zeros((crop_size, row_count, channels), jnp.float32),
        jnp.zeros((num_heads, crop_size, crop_size), jnp.float32),
        jnp.zeros((channels, 4 * channels), jnp.float32),
        jnp.zeros((channels,), jnp.float32),
        jnp.zeros((channels, channels), jnp.float32),
    )
    dn_cols, bias_grad, proj_grad, gate_grad, out_grad = lax.fori_loop(
        0, block_count, block_step, init
    )
    grad_owned = lax.psum_scatter(
        bias_grad.astype(jnp.bfloat16), "row", scatter_dimension=1, tiled=True
    )
    d_norm_side = jnp.einsum("hki,ch->kic", grad_owned, w_bias, preferred_element_type=jnp.float32)
    bias_w_grad = jnp.einsum("kic,hki->ch", normed, grad_owned, preferred_element_type=jnp.float32)
    main_rows = lax.all_to_all(
        dn_cols.astype(jnp.bfloat16), "row", split_axis=0, concat_axis=1, tiled=True
    ).astype(dn_cols.dtype)
    d_norm_all = (main_rows + d_norm_side).astype(jnp.bfloat16).astype(jnp.float32)
    dz_rows, gain_side, shift_side = side_back(d_norm_all)
    pair_grad = dz_rows.astype(jnp.bfloat16)
    totals = lax.psum(
        (proj_grad, gate_grad, bias_w_grad, out_grad, gain_side, shift_side), ("dp", "row")
    )
    return (
        pair_grad[None],
        totals[0] / crop_size,
        totals[1] / crop_size,
        totals[2] / crop_size,
        totals[3] / crop_size,
        totals[4] / crop_size,
        totals[5] / crop_size,
    )


def solution(mesh):
    placed = (
        P("dp", "row", None, None),
        P("dp", "row", None, None),
        P("dp"),
        P(),
        P(),
        P(),
        P(),
        P(),
        P(),
    )
    return jax.shard_map(
        body,
        mesh=mesh,
        in_specs=placed,
        out_specs=(P("dp", "row", None, None), P(), P(), P(), P(), P(), P()),
        check_vma=False,
    )
```

profile of v0, /device:TPU:1, one launch (start us, length us, event | category | flops | bytes accessed | tf_op | source)
XLA Modules:
  0.0 960.5 jit_solution(7924106332688091682)
XLA Ops:
  13.9 7.3 all-to-all-start.1
  27.7 23.9 %all-to-all-done.1 = bf16[24,384,128]{2,0,1:T(8,128)(2,1)} async-done(((bf16[24,384,128]{2,0,1:T(8,128)(2,1)}), bf16[24,384,128]{2,0,1:T(8,128)(2,1)}, u32[]{:S(2)}, u32[]{:S(2)}) %all-to-all-start.1) | async-done | bytes 2359328 | tf_op jit(solution)/shard_map/all_to_all | solution.py:34
  57.6 7.1 convolution_convert_fusion.1
  69.2 19.2 %all-to-all-done = bf16[24,384,128]{2,0,1:T(8,128)(2,1)} async-done(((bf16[24,384,128]{2,0,1:T(8,128)(2,1)}), bf16[24,384,128]{2,0,1:T(8,128)(2,1)}, u32[]{:S(2)}, u32[]{:S(2)}) %all-to-all-start) | async-done | bytes 2359328 | tf_op jit(solution)/shard_map/all_to_all | solution.py:33
  93.8 14.8 %all-gather.2.cloned.1.call-done = bf16[4,384,384]{2,1,0:T(8,128)(2,1)} async-done(((bf16[4,24,384]{2,1,0:T(8,128)(2,1)}), bf16[4,384,384]{2,1,0:T(8,128)(2,1)}) %all-gather.2.cloned.1.call-update) | async-done | bytes 1179664 | tf_op jit(solution)/shard_map/all_gather | solution.py:41
  110.3 528.2 %while.22 = (s32[]{:T(128)}, bf16[384,24,128]{2,1,0:T(8,128)(2,1)}, f32[4,384,384]{2,1,0:T(8,128)}, f32[128,512]{1,0:T(8,128)}, f32[128]{0:T(128)}, /*index=5*/f...) while((s32[]{:T(128)}, bf16[384,24,128]{2,1,0:T(8,128)(2,1)}, ...), condition=%wide.region_9.10_spmd.clone, body=%wide.region_2.9_spmd.clone.sunk | while | flops 1665619968 | bytes 183881136 | solution.py:115
  131.6 14.6 %multiply_reduce_fusion.5 = (f32[4,4,384]{2,1,0:T(4,128)}, f32[4,4,384,384]{3,2,1,0:T(8,128)}, f32[4,4,384,384]{3,2,1,0:T(8,128)}) fusion(f32[4,4,384]{2,1,0:T(4,128)} %get-tuple-element.538, f32[4,4,384,384]{3,2,1,0:T(8,128)} %get-tuple-element.539, f32[4,384,384]{2,1,0:T(8,128)S(1)} %convert_element_type.266, ...), kind=kOutput, calls=%fused_computation.2.clone.1 | convolution fusion | flops 162785280 | bytes 31506816 | tf_op jit(solution)/shard_map/while/body/eval_jaxpr/ibhd,kbhd->bhki/dot_general | solution.py:78
  146.2 11.0 %fusion.136 = (f32[4,384,384]{2,1,0:T(8,128)S(1)}, bf16[4,4,384,384]{3,2,1,0:T(8,128)(2,1)}) fusion(f32[4,4,384,384]{3,2,1,0:T(8,128)} %get-tuple-element.541, f32[4,4,384,384]{3,2,1,0:T(8,128)} %get-tuple-element.543, f32[4,4,384]{2,1,0:T(4,128)} %get-tuple-element.544), kind=kLoop, calls=%fused_computation.6.clone.1 | loop fusion | flops 8847360 | bytes 25976832 | tf_op jit(solution)/shard_map/while/body/eval_jaxpr/reduce_sum | solution.py:102
  219.6 14.6 %multiply_reduce_fusion.5 = (f32[4,4,384]{2,1,0:T(4,128)}, f32[4,4,384,384]{3,2,1,0:T(8,128)}, f32[4,4,384,384]{3,2,1,0:T(8,128)}) fusion(f32[4,4,384]{2,1,0:T(4,128)} %get-tuple-element.538, f32[4,4,384,384]{3,2,1,0:T(8,128)} %get-tuple-element.539, f32[4,384,384]{2,1,0:T(8,128)S(1)} %convert_element_type.266, ...), kind=kOutput, calls=%fused_computation.2.clone.1 | convolution fusion | flops 162785280 | bytes 31506816 | tf_op jit(solution)/shard_map/while/body/eval_jaxpr/ibhd,kbhd->bhki/dot_general | solution.py:78
  234.2 11.0 %fusion.136 = (f32[4,384,384]{2,1,0:T(8,128)S(1)}, bf16[4,4,384,384]{3,2,1,0:T(8,128)(2,1)}) fusion(f32[4,4,384,384]{3,2,1,0:T(8,128)} %get-tuple-element.541, f32[4,4,384,384]{3,2,1,0:T(8,128)} %get-tuple-element.543, f32[4,4,384]{2,1,0:T(4,128)} %get-tuple-element.544), kind=kLoop, calls=%fused_computation.6.clone.1 | loop fusion | flops 8847360 | bytes 25976832 | tf_op jit(solution)/shard_map/while/body/eval_jaxpr/reduce_sum | solution.py:102
  257.7 6.2 fusion.135
  307.6 14.6 %multiply_reduce_fusion.5 = (f32[4,4,384]{2,1,0:T(4,128)}, f32[4,4,384,384]{3,2,1,0:T(8,128)}, f32[4,4,384,384]{3,2,1,0:T(8,128)}) fusion(f32[4,4,384]{2,1,0:T(4,128)} %get-tuple-element.538, f32[4,4,384,384]{3,2,1,0:T(8,128)} %get-tuple-element.539, f32[4,384,384]{2,1,0:T(8,128)S(1)} %convert_element_type.266, ...), kind=kOutput, calls=%fused_computation.2.clone.1 | convolution fusion | flops 162785280 | bytes 31506816 | tf_op jit(solution)/shard_map/while/body/eval_jaxpr/ibhd,kbhd->bhki/dot_general | solution.py:78
  322.2 11.0 %fusion.136 = (f32[4,384,384]{2,1,0:T(8,128)S(1)}, bf16[4,4,384,384]{3,2,1,0:T(8,128)(2,1)}) fusion(f32[4,4,384,384]{3,2,1,0:T(8,128)} %get-tuple-element.541, f32[4,4,384,384]{3,2,1,0:T(8,128)} %get-tuple-element.543, f32[4,4,384]{2,1,0:T(4,128)} %get-tuple-element.544), kind=kLoop, calls=%fused_computation.6.clone.1 | loop fusion | flops 8847360 | bytes 25976832 | tf_op jit(solution)/shard_map/while/body/eval_jaxpr/reduce_sum | solution.py:102
  395.6 14.6 %multiply_reduce_fusion.5 = (f32[4,4,384]{2,1,0:T(4,128)}, f32[4,4,384,384]{3,2,1,0:T(8,128)}, f32[4,4,384,384]{3,2,1,0:T(8,128)}) fusion(f32[4,4,384]{2,1,0:T(4,128)} %get-tuple-element.538, f32[4,4,384,384]{3,2,1,0:T(8,128)} %get-tuple-element.539, f32[4,384,384]{2,1,0:T(8,128)S(1)} %convert_element_type.266, ...), kind=kOutput, calls=%fused_computation.2.clone.1 | convolution fusion | flops 162785280 | bytes 31506816 | tf_op jit(solution)/shard_map/while/body/eval_jaxpr/ibhd,kbhd->bhki/dot_general | solution.py:78
  410.2 11.0 %fusion.136 = (f32[4,384,384]{2,1,0:T(8,128)S(1)}, bf16[4,4,384,384]{3,2,1,0:T(8,128)(2,1)}) fusion(f32[4,4,384,384]{3,2,1,0:T(8,128)} %get-tuple-element.541, f32[4,4,384,384]{3,2,1,0:T(8,128)} %get-tuple-element.543, f32[4,4,384]{2,1,0:T(4,128)} %get-tuple-element.544), kind=kLoop, calls=%fused_computation.6.clone.1 | loop fusion | flops 8847360 | bytes 25976832 | tf_op jit(solution)/shard_map/while/body/eval_jaxpr/reduce_sum | solution.py:102
  483.6 14.6 %multiply_reduce_fusion.5 = (f32[4,4,384]{2,1,0:T(4,128)}, f32[4,4,384,384]{3,2,1,0:T(8,128)}, f32[4,4,384,384]{3,2,1,0:T(8,128)}) fusion(f32[4,4,384]{2,1,0:T(4,128)} %get-tuple-element.538, f32[4,4,384,384]{3,2,1,0:T(8,128)} %get-tuple-element.539, f32[4,384,384]{2,1,0:T(8,128)S(1)} %convert_element_type.266, ...), kind=kOutput, calls=%fused_computation.2.clone.1 | convolution fusion | flops 162785280 | bytes 31506816 | tf_op jit(solution)/shard_map/while/body/eval_jaxpr/ibhd,kbhd->bhki/dot_general | solution.py:78
  498.2 11.0 %fusion.136 = (f32[4,384,384]{2,1,0:T(8,128)S(1)}, bf16[4,4,384,384]{3,2,1,0:T(8,128)(2,1)}) fusion(f32[4,4,384,384]{3,2,1,0:T(8,128)} %get-tuple-element.541, f32[4,4,384,384]{3,2,1,0:T(8,128)} %get-tuple-element.543, f32[4,4,384]{2,1,0:T(4,128)} %get-tuple-element.544), kind=kLoop, calls=%fused_computation.6.clone.1 | loop fusion | flops 8847360 | bytes 25976832 | tf_op jit(solution)/shard_map/while/body/eval_jaxpr/reduce_sum | solution.py:102
  571.7 14.6 %multiply_reduce_fusion.5 = (f32[4,4,384]{2,1,0:T(4,128)}, f32[4,4,384,384]{3,2,1,0:T(8,128)}, f32[4,4,384,384]{3,2,1,0:T(8,128)}) fusion(f32[4,4,384]{2,1,0:T(4,128)} %get-tuple-element.538, f32[4,4,384,384]{3,2,1,0:T(8,128)} %get-tuple-element.539, f32[4,384,384]{2,1,0:T(8,128)S(1)} %convert_element_type.266, ...), kind=kOutput, calls=%fused_computation.2.clone.1 | convolution fusion | flops 162785280 | bytes 31506816 | tf_op jit(solution)/shard_map/while/body/eval_jaxpr/ibhd,kbhd->bhki/dot_general | solution.py:78
  586.3 11.0 %fusion.136 = (f32[4,384,384]{2,1,0:T(8,128)S(1)}, bf16[4,4,384,384]{3,2,1,0:T(8,128)(2,1)}) fusion(f32[4,4,384,384]{3,2,1,0:T(8,128)} %get-tuple-element.541, f32[4,4,384,384]{3,2,1,0:T(8,128)} %get-tuple-element.543, f32[4,4,384]{2,1,0:T(4,128)} %get-tuple-element.544), kind=kLoop, calls=%fused_computation.6.clone.1 | loop fusion | flops 8847360 | bytes 25976832 | tf_op jit(solution)/shard_map/while/body/eval_jaxpr/reduce_sum | solution.py:102
  646.9 148.3 %all-reduce.4.cloned.1.call-done = (f32[128,512]{1,0:T(8,128)}, f32[128,128]{1,0:T(8,128)}) async-done(((f32[128,512]{1,0:T(8,128)}, f32[128,128]{1,0:T(8,128)}), (f32[128,512]{1,0:T(8,128)}, f32[128,128]{1,0:T(8,128)})) %all-reduce.4.cloned.1.call-update) | async-done | bytes 327696 | tf_op jit(solution)/shard_map/psum | solution.py:129
  802.7 51.1 %reduce-scatter.4.cloned.1.call-done = bf16[24,1536]{1,0:T(8,128)(2,1)} async-done(((bf16[384,1536]{1,0:T(8,128)(2,1)}), bf16[24,1536]{1,0:T(8,128)(2,1)}) %reduce-scatter.4.cloned.1.call-update) | async-done | bytes 73744
  862.8 6.7 fusion.49
  869.5 68.1 %all-reduce = (f32[128]{0:T(128)S(1)}, f32[128,4]{0,1:T(4,128)S(1)}, f32[128]{0:T(128)S(1)}, f32[128]{0:T(128)S(1)}) all-reduce(f32[128]{0:T(128)S(1)} %copy-done.29, f32[128,4]{0,1:T(4,128)S(1)} %fusion.63, f32[128]{0:T(128)S(1)} %get-tuple-element.356, f32[128]{0:T(128)S(1)} %get-tuple-element.359), channel_id=1, replica_groups=mesh['dp'=8,'row'=16] {'dp','row'}, use_global_device_ids=true, to_apply=%region_15.16 | all-reduce | flops 896 | bytes 7168 | tf_op jit(solution)/shard_map/psum | solution.py:129
  943.1 10.3 %fusion.56 = bf16[1,24,384,128]{3,2,1,0:T(8,128)(2,1)} fusion(bf16[24,384,128]{2,1,0:T(8,128)(2,1)} %copy-done.10, f32[24,384]{1,0:T(8,128)S(1)} %add_multiply_fusion, f32[24,384]{1,0:T(8,128)S(1)} %multiply_multiply_fusion, f32[24,384]{1,0:T(8,128)S(1)} %copy-done.24, f32[128]{0:T(128)} %param.14, f32[24,384]{1,0:T(8,128)S(1)} %copy-done.21, ...), kind=kLoop, calls=%fused_computation.82 | loop fusion | flops 10616832 | bytes 7225856 | tf_op jit(solution)/shard_map/broadcast_in_dim | solution.py:133
  (504 shorter events, 427.7 us)
Async XLA Ops:
  7.2 50.4 %copy-start = (bf16[128,4]{0,1:T(4,128)(2,1)S(1)}, bf16[128,4]{0,1:T(4,128)(2,1)}, u32[]{:S(2)}) copy-start(bf16[128,4]{0,1:T(4,128)(2,1)} %param.18) | copy-start | bytes 3076
  8.0 13.3 %copy-start.7 = (bf16[1,24,384,128]{3,2,1,0:T(8,128)(2,1)S(1)}, bf16[1,24,384,128]{3,2,1,0:T(8,128)(2,1)}, u32[]{:S(2)}) copy-start(bf16[1,24,384,128]{3,2,1,0:T(8,128)(2,1)} %param.11) | copy-start | bytes 7077892
  13.9 37.7 %all-to-all-start.1 = ((bf16[24,384,128]{2,0,1:T(8,128)(2,1)}), bf16[24,384,128]{2,0,1:T(8,128)(2,1)}, u32[]{:S(2)}, u32[]{:S(2)}) async-start(bf16[24,384,128]{2,0,1:T(8,128)(2,1)} %bitcast_select_fusion), calls=%async_computation.1 | async-start | bytes 4718592 | tf_op jit(solution)/shard_map/all_to_all | solution.py:34
  24.9 39.8 %copy-start.20 = (f32[24,384]{1,0:T(8,128)}, f32[24,384]{1,0:T(8,128)S(1)}, u32[]{:S(2)}) copy-start(f32[24,384]{1,0:T(8,128)S(1)} %broadcast_multiply_fusion.3) | copy-start | bytes 110596
  27.7 37.0 %copy-start.25 = (f32[24,384]{1,0:T(8,128)}, f32[24,384]{1,0:T(8,128)S(1)}, u32[]{:S(2)}) copy-start(f32[24,384]{1,0:T(8,128)S(1)} %fusion.47) | copy-start | bytes 110596
  51.6 36.7 %all-to-all-start = ((bf16[24,384,128]{2,0,1:T(8,128)(2,1)}), bf16[24,384,128]{2,0,1:T(8,128)(2,1)}, u32[]{:S(2)}, u32[]{:S(2)}) async-start(bf16[24,384,128]{2,0,1:T(8,128)(2,1)} %copy.83), calls=%async_computation | async-start | bytes 4718592 | tf_op jit(solution)/shard_map/all_to_all | solution.py:33
  57.5 51.1 %all-gather.2.cloned.1.call-start = ((), (), s32[]{:S(2)}) async-start(), calls=%async_computation.4 | async-start | bytes 1253376 | tf_op jit(solution)/shard_map/all_gather | solution.py:41
  57.6 11.6 %copy-start.23 = (f32[24,384]{1,0:T(8,128)}, f32[24,384]{1,0:T(8,128)S(1)}, u32[]{:S(2)}) copy-start(f32[24,384]{1,0:T(8,128)S(1)} %fusion.68) | copy-start | bytes 110596
  65.4 729.9 %all-reduce.4.cloned.1.call-start = ((), (), s32[]{:S(2)}) async-start(), calls=%async_computation.6 | async-start | bytes 655360 | tf_op jit(solution)/shard_map/psum | solution.py:129
  91.2 19.1 %copy-start.16 = (bf16[128,512]{1,0:T(8,128)(2,1)S(1)}, bf16[128,512]{1,0:T(8,128)(2,1)}, u32[]{:S(2)}) copy-start(bf16[128,512]{1,0:T(8,128)(2,1)} %param.16) | copy-start | bytes 393220
  91.2 19.1 %copy-start.30 = (f32[128]{0:T(128)S(1)}, f32[128]{0:T(128)}, u32[]{:S(2)}) copy-start(f32[128]{0:T(128)} %param.17) | copy-start | bytes 1540
  169.8 8.2 copy-start.9
  257.7 8.2 copy-start.9
  345.8 8.2 copy-start.9
  433.8 8.2 copy-start.9
  521.8 8.2 copy-start.9
  609.8 8.2 copy-start.9
  638.4 215.4 %reduce-scatter.4.cloned.1.call-start = ((), (), s32[]{:S(2)}) async-start(), calls=%async_computation.5 | async-start | bytes 1253376
  642.5 155.9 %all-to-all-start.2 = ((bf16[384,24,128]{2,1,0:T(8,128)(2,1)}), bf16[384,24,128]{2,1,0:T(8,128)(2,1)}, u32[]{:S(2)}, u32[]{:S(2)}) async-start(bf16[384,24,128]{2,1,0:T(8,128)(2,1)} %get-tuple-element.649), calls=%async_computation.2 | async-start | bytes 4718592 | tf_op jit(solution)/shard_map/all_to_all | solution.py:123
  646.9 207.8 %copy-start.8 = (bf16[1,24,384,128]{3,2,1,0:T(8,128)(2,1)S(1)}, bf16[1,24,384,128]{3,2,1,0:T(8,128)(2,1)}, u32[]{:S(2)}) copy-start(bf16[1,24,384,128]{3,2,1,0:T(8,128)(2,1)} %param.11) | copy-start | bytes 7077892
  646.9 207.8 %copy-start.21 = (f32[24,384]{1,0:T(8,128)S(1)}, f32[24,384]{1,0:T(8,128)}, u32[]{:S(2)}) copy-start(f32[24,384]{1,0:T(8,128)} %copy-done.20) | copy-start | bytes 110596
  646.9 207.8 %copy-start.24 = (f32[24,384]{1,0:T(8,128)S(1)}, f32[24,384]{1,0:T(8,128)}, u32[]{:S(2)}) copy-start(f32[24,384]{1,0:T(8,128)} %copy-done.23) | copy-start | bytes 110596
  860.3 9.1 copy-start.29
  860.3 78.4 %copy-start.26 = (f32[24,384]{1,0:T(8,128)S(1)}, f32[24,384]{1,0:T(8,128)}, u32[]{:S(2)}) copy-start(f32[24,384]{1,0:T(8,128)} %copy-done.25) | copy-start | bytes 110596
  (104 other events, 375.9 us)
Sparse Core Ops, SparseCore 0:
  65.5 42.9 all-gather.1
  638.6 156.6 all-reduce.3
  797.7 56.1 reduce-scatter.3
where the time goes:
time: 965 us; the launch traced here: 961 us
  matrix products  308 us (32%)
  waiting for transfers between devices  257 us (27%)
  local copies, waits for them, and re-layouts  152 us (16%)
  other arithmetic  141 us (15%)
  blocking collectives  68.1 us (7%)
  starting transfers between devices  17.8 us (2%)
  between operations  14.7 us (2%)
    psum x1, waiting for transfers between devices, body(): lax.psum((proj_grad, gate_grad, bias_w_grad, out_grad, gain_side, shift_s...  148 us
    dot_general x6, matrix products, block_step(): jnp.einsum('ibhd,kbhd->bhki', d_attended, value_blk, preferred_element_ty...  87.7 us
    psum x1, blocking collectives, body(): lax.psum((proj_grad, gate_grad, bias_w_grad, out_grad, gain_side, shift_s...  68.1 us
    reduce_sum x6, other arithmetic, block_step(): bias_grad = bias_grad + jnp.sum(d_scores, axis=0)  65.9 us
    unnamed x4, waiting for transfers between devices  51.1 us
    concatenate x24, local copies, waits for them, and re-layouts, block_step(): jnp.concatenate(pieces, axis=-1).astype(jnp.bfloat16)  46.9 us
    dot_general x6, matrix products, block_step(): jnp.einsum('bhki,ibhd->kbhd', weights_b, d_attended, preferred_element_ty...  37.2 us
    dot_general x6, matrix products, block_step(): jnp.einsum('bhki,kbhd->ibhd', weights_b, value_blk, preferred_element_typ...  34.1 us
  transfers between devices with their start and end apart: 6, of which 5 were waited for; matrix products, arithmetic and copies ran while one was open for 4% of the time, Pallas kernels for 0%

commit v1 on v0

v1 whole, which is shorter than its diff:
```python
import functools
import math

import jax
import jax.numpy as jnp
from jax import lax
from jax.experimental import pallas as pl
from jax.experimental.pallas import tpu as pltpu
from jax.sharding import PartitionSpec as P

F32, BF = jnp.float32, jnp.bfloat16
EPSILON = 1e-05
LOG2E = 1.4426950408889634
LN2 = 0.6931471805599453
NN = (((1,), (0,)), ((), ()))
NT = (((1,), (1,)), ((), ()))
TN = (((0,), (0,)), ((), ()))
MIB = 2**20
DEAD = -1e30
CHUNKS = (12, 12)


def dot(a, b, dims=NN):
    return lax.dot_general(a, b, dims, preferred_element_type=F32)


def norm_parts(x):
    centered = x - jnp.mean(x, axis=-1, keepdims=True)
    scale = lax.rsqrt(jnp.mean(centered * centered, axis=-1, keepdims=True) + EPSILON)
    return centered * scale, scale


def fold_rows(a):
    return jnp.sum(a.reshape(a.shape[0] // 8, 8, a.shape[1]), axis=0)


def logits_kernel(pair_ref, gain_ref, shift_ref, wbt_ref, out_ref):
    rows, size, channels = pair_ref.shape
    for r in range(rows):
        xhat, _ = norm_parts(pair_ref[r].astype(F32))
        normed = (xhat * gain_ref[...] + shift_ref[...]).astype(BF)
        out_ref[:, r, :] = dot(wbt_ref[...], normed, NT)


def columns_kernel(heads, first, last, col0, len_ref, own_ref, pair_ref, cot_ref, *refs):
    if first:
        bias_in, refs = refs[0], refs[1:]
    else:
        (bias_ref, bacc_in, wacc_in, sacc_in), refs = refs[:4], refs[4:]
    gain_ref, shift_ref, wp_ref, wpt_ref, gb_ref, wot_ref = refs[:6]
    dn_ref, bout_ref, wacc_ref, sacc_ref = refs[6:10]
    refs = refs[10:]
    if first:
        bias_ref, refs = refs[0], refs[1:]
    e_ref, ds_ref, kbd, vaug = refs[:4]
    bacc_ref = refs[4] if last else bout_ref
    step = pl.program_id(0)
    n, channels = bacc_ref.shape[0], wp_ref.shape[0]
    size = channels // heads
    lane = lax.broadcasted_iota(jnp.int32, (1, channels), 1)
    masks = [jnp.where(lane // size == h, 1.0, 0.0).astype(BF) for h in range(heads)]
    length = len_ref[0]

    @pl.when(step == 0)
    def _():
        if first:
            kpos = lax.broadcasted_iota(jnp.int32, (1, n), 1)
            for h in range(heads):
                plane = bias_in[:, h].astype(F32).reshape(n, n)
                bias_ref[:, h * n : (h + 1) * n] = jnp.where(kpos < length, plane.T * LOG2E, DEAD)
            bacc_ref[...] = jnp.zeros_like(bacc_ref)
            wacc_ref[...] = jnp.zeros_like(wacc_ref)
            sacc_ref[...] = jnp.zeros_like(sacc_ref)
        else:
            bacc_ref[...] = bacc_in[...]
            wacc_ref[...] = wacc_in[...]
            sacc_ref[...] = sacc_in[...]
        for h in range(heads):
            vaug[h * n : (h + 1) * n, channels:] = jnp.broadcast_to(masks[h], (n, channels))

    xhat, _ = norm_parts(pair_ref[...].astype(F32).reshape(n, channels))
    normed_f = xhat * gain_ref[...] + shift_ref[...]
    proj = dot(normed_f.astype(BF), wp_ref[...])
    q_f = proj[:, :channels] * (LOG2E / math.sqrt(size))
    k = proj[:, channels : 2 * channels].astype(BF)
    v = proj[:, 2 * channels : 3 * channels].astype(BF)
    gate = jax.nn.sigmoid(proj[:, 3 * channels :] + gb_ref[...])
    for h in range(heads):
        kbd[h * n : (h + 1) * n, :] = k * masks[h]
        vaug[h * n : (h + 1) * n, :channels] = v * masks[h]
    live = lax.broadcasted_iota(jnp.int32, (n, 1), 0) < length
    live = live & (own_ref[0] + col0 + step < length)
    cot = jnp.where(live, cot_ref[...].astype(F32).reshape(n, channels), 0.0).astype(BF)
    d_out = dot(cot, wot_ref[...])

    e_ref[...] = jnp.exp2(dot(q_f.astype(BF), kbd[...], NT) + bias_ref[...]).astype(BF)
    summed = dot(e_ref[...], vaug[...])
    recip = 1.0 / summed[:, channels:]
    att = summed[:, :channels] * recip
    d_att = d_out * gate
    d_gate = d_att * att * (1.0 - gate)
    d_att_b = (d_att * recip).astype(BF)
    d_att_f = d_att_b.astype(F32)
    terms = d_att_f * att
    terms_hi = terms.astype(BF)
    terms_lo = (terms - terms_hi.astype(F32)).astype(BF)
    gi = lax.broadcasted_iota(jnp.int32, (2 * channels, channels), 0) % channels
    gj = lax.broadcasted_iota(jnp.int32, (2 * channels, channels), 1)
    group = jnp.where((gi // size == gj // size) & (gj % size < 2), -1.0, 0.0).astype(BF)
    row_dot = dot(jnp.concatenate([terms_hi, terms_lo], axis=1), group)
    row_hi = row_dot.astype(BF).astype(F32)
    row_lanes = jnp.where(lane % size == 0, row_hi, row_dot - row_hi).astype(BF)
    ds = e_ref[...].astype(F32) * dot(jnp.concatenate([d_att_b, row_lanes], axis=1), vaug[...], NT)
    bacc_ref[...] += ds
    ds_ref[...] = ds.astype(BF)
    d_query = dot(ds_ref[...], kbd[...]) * (1.0 / math.sqrt(size))
    q_t, d_att_t = q_f.T.astype(BF), d_att_f.T.astype(BF)
    dk_t, dv_t = [], []
    for p in range(heads // 2):
        rows = slice(2 * p * size, 2 * (p + 1) * size)
        lanes = slice(2 * p * n, 2 * (p + 1) * n)
        both = dot(q_t[rows], ds_ref[:, lanes])
        dk_t += [both[:size, :n], both[size:, n:]]
        both = dot(d_att_t[rows], e_ref[:, lanes])
        dv_t += [both[:size, :n], both[size:, n:]]
    d_key = (jnp.concatenate(dk_t, axis=0) * LN2).T
    d_value = jnp.concatenate(dv_t, axis=0).T
    d_proj = jnp.concatenate([g.astype(BF) for g in (d_query, d_key, d_value, d_gate)], axis=1)
    dn = dot(d_proj, wpt_ref[...])
    dn_ref[...] = dn.reshape(dn_ref.shape).astype(BF)
    gated = gate * att
    wacc_ref[:, : 4 * channels] += dot(normed_f.T.astype(BF), d_proj)
    wacc_ref[:, 4 * channels :] += dot(gated.T.astype(BF), cot)
    sacc_ref[0] += fold_rows(d_gate)
    sacc_ref[1] += fold_rows(dn * xhat)
    sacc_ref[2] += fold_rows(dn)

    if last:

        @pl.when(step == pl.num_programs(0) - 1)
        def _():
            for h in range(heads):
                plane = bacc_ref[:, h * n : (h + 1) * n].T
                bout_ref[:, h] = plane.reshape(bout_ref.shape[0], -1, n).astype(BF)


def whole(shape):
    return pl.BlockSpec(shape, lambda j: (0,) * len(shape))


def columns_call(first, last, col0, length, own, moved, state, weights, heads):
    src, _, cols, rows, channels = moved.shape
    n = src * rows
    smem = pl.BlockSpec(memory_space=pltpu.SMEM)
    plane = jax.ShapeDtypeStruct((n, heads * n), F32)
    outs = [
        jax.ShapeDtypeStruct((src, cols, rows, channels), BF),
        jax.ShapeDtypeStruct((src, heads, rows, n), BF) if last else plane,
        jax.ShapeDtypeStruct((channels, 5 * channels), F32),
        jax.ShapeDtypeStruct((3, 8, channels), F32),
    ] + ([plane] if first else [])
    cells = (src, None, None, rows, channels)
    return pl.pallas_call(
        functools.partial(columns_kernel, heads, first, last, col0),
        grid=(cols,),
        in_specs=[
            smem,
            smem,
            pl.BlockSpec(cells, lambda j: (0, 0, j, 0, 0)),
            pl.BlockSpec(cells, lambda j: (0, 1, j, 0, 0)),
        ]
        + [whole(a.shape) for a in (*state, *weights)],
        out_specs=[pl.BlockSpec((src, None, rows, channels), lambda j: (0, j, 0, 0))]
        + [whole(o.shape) for o in outs[1:]],
        out_shape=outs,
        scratch_shapes=[
            pltpu.VMEM((n, heads * n), BF),
            pltpu.VMEM((n, heads * n), BF),
            pltpu.VMEM((heads * n, channels), BF),
            pltpu.VMEM((heads * n, 2 * channels), BF),
        ]
        + ([pltpu.VMEM((n, heads * n), F32)] if last else []),
        compiler_params=pltpu.CompilerParams(
            vmem_limit_bytes=56 * MIB, dimension_semantics=("arbitrary",)
        ),
        cost_estimate=pl.CostEstimate(
            flops=cols * heads * n * n * 400, bytes_accessed=cols * n * channels * 6, transcendentals=0
        ),
    )(length, own, moved, moved, *state, *weights)


def side_kernel(pair_ref, parts_ref, gain_ref, shift_ref, sum_ref, stat_ref):
    rows = pair_ref.shape[0]
    heads = parts_ref.shape[1]
    total = jnp.sum(parts_ref[...].astype(F32), axis=0).astype(BF).astype(F32)
    sum_ref[...] = total
    stats = None
    flat = None
    for r in range(rows):
        xhat, _ = norm_parts(pair_ref[r].astype(F32))
        normed = (xhat * gain_ref[...] + shift_ref[...]).astype(BF)
        own = total[:, r, :].astype(BF)
        one = dot(own, jnp.concatenate([normed, xhat.astype(BF)], axis=1))
        stats = one if stats is None else stats + one
        flat = total[:, r, :] if flat is None else flat + total[:, r, :]
    channels = pair_ref.shape[2]
    stat_ref[:, : 2 * channels] = stats
    stat_ref[:, 2 * channels :] = jnp.broadcast_to(
        jnp.sum(flat, axis=1, keepdims=True), (heads, channels)
    )


def norm_back_kernel(counts, pair_ref, sums_ref, gain_ref, wbt_ref, *refs):
    out_ref = refs[-1]
    rows, cols, channels = pair_ref.shape
    pieces = []
    for s in range(refs[0].shape[0]):
        for ref in refs[:-1]:
            pieces.append(ref[s].astype(F32))
    main = jnp.swapaxes(jnp.concatenate(pieces, axis=0), 0, 1).reshape(rows * cols, channels)
    side = dot(sums_ref[...].astype(BF), wbt_ref[...], TN)
    d_normed = (main + side).astype(BF).astype(F32)
    xhat, scale = norm_parts(pair_ref[...].astype(F32).reshape(rows * cols, channels))
    g = d_normed * gain_ref[...]
    dx = scale * (
        g
        - jnp.mean(g, axis=-1, keepdims=True)
        - xhat * jnp.mean(g * xhat, axis=-1, keepdims=True)
    )
    out_ref[...] = dx.reshape(rows, cols, channels).astype(BF)


def body(pair_rep, grad_out, crop_len, ln_gain, ln_bias, w_proj, gate_bias, w_bias, w_out):
    pair, cot = pair_rep[0], grad_out[0]
    rows, n, channels = pair.shape
    heads = w_bias.shape[1]
    src = n // rows
    everywhere = ("dp", "row")
    devices = lax.axis_size("dp") * lax.axis_size("row")
    own = (lax.axis_index("row") * rows).astype(jnp.int32).reshape(1)
    gain, shift = ln_gain.reshape(1, -1), ln_bias.reshape(1, -1)
    wbt = jnp.zeros((8, channels), BF).at[:heads].set(w_bias.T)
    weights = (gain, shift, w_proj, w_proj.T, gate_bias.reshape(1, -1), w_out.T)

    def exchange(a, axis="row"):
        return lax.all_to_all(a, axis, 0, 0)

    half = 8
    logits = pl.pallas_call(
        logits_kernel,
        grid=(rows // half,),
        in_specs=[
            pl.BlockSpec((half, n, channels), lambda j: (j, 0, 0)),
            whole(gain.shape),
            whole(shift.shape),
            whole(wbt.shape),
        ],
        out_specs=pl.BlockSpec((8, half, n), lambda j: (0, j, 0)),
        out_shape=jax.ShapeDtypeStruct((8, rows, n), F32),
    )(pair, gain, shift, wbt)
    bias = exchange(jnp.broadcast_to(logits[None, :heads].astype(BF), (src, heads, rows, n)))

    both = jnp.stack([pair, cot]).reshape(2, rows, src, rows, channels)
    starts = [sum(CHUNKS[:c]) for c in range(len(CHUNKS))]
    moved = [
        exchange(both[:, :, :, s : s + w].transpose(2, 0, 3, 1, 4)) for s, w in zip(starts, CHUNKS)
    ]
    state, back = (bias,), []
    for c, (s, piece) in enumerate(zip(starts, moved)):
        first, last = c == 0, c == len(CHUNKS) - 1
        dn, bacc, wacc, sacc, *rest = columns_call(
            first, last, s, crop_len, own, piece, state, weights, heads
        )
        plane = rest[0] if first else state[0]
        state = (plane, bacc, wacc, sacc)
        if not last:
            back.append(exchange(dn))
    parts = exchange(bacc)
    back.append(exchange(dn))
    share = exchange(wacc.reshape(devices, -1, channels), everywhere)

    sums, stats = pl.pallas_call(
        side_kernel,
        out_shape=[
            jax.ShapeDtypeStruct((heads, rows, n), F32),
            jax.ShapeDtypeStruct((heads, 3 * channels), F32),
        ],
        compiler_params=pltpu.CompilerParams(vmem_limit_bytes=40 * MIB),
    )(pair, parts, gain, shift)

    wide = w_bias.T.astype(F32)
    extra_gain = jnp.sum(wide * stats[:, channels : 2 * channels], axis=0)
    extra_shift = jnp.sum(wide * stats[:, 2 * channels :], axis=0)
    small = jnp.sum(sacc, axis=1) + jnp.stack([jnp.zeros_like(extra_gain), extra_gain, extra_shift])
    small = jnp.concatenate([small, stats[:, :channels]], axis=0)
    reduced = jnp.sum(share, axis=0)
    told = jnp.concatenate([reduced, small], axis=0)
    told = exchange(jnp.broadcast_to(told[None], (devices, *told.shape)), everywhere)
    held = reduced.shape[0]
    w_total = told[:, :held].reshape(channels, 5 * channels) / n
    s_total = jnp.sum(told[:, held:], axis=0) / n

    block = 2
    tile = block * rows
    folded = sums.reshape(heads, rows, n // tile, tile).transpose(2, 0, 1, 3)
    folded = folded.reshape(n // tile, heads, rows * tile)
    folded = jnp.pad(folded, ((0, 0), (0, 8 - heads), (0, 0)))
    cells = pl.BlockSpec((rows, tile, channels), lambda j: (0, j, 0))
    pair_grad = pl.pallas_call(
        functools.partial(norm_back_kernel, CHUNKS),
        grid=(n // tile,),
        in_specs=[
            cells,
            pl.BlockSpec((None, 8, rows * tile), lambda j: (j, 0, 0)),
            whole(gain.shape),
            whole(wbt.shape),
        ]
        + [pl.BlockSpec((block, w, rows, channels), lambda j: (j, 0, 0, 0)) for w in CHUNKS],
        out_specs=cells,
        out_shape=jax.ShapeDtypeStruct(pair.shape, BF),
        compiler_params=pltpu.CompilerParams(vmem_limit_bytes=40 * MIB),
    )(pair, folded, gain, wbt, *back)
    return (
        pair_grad[None],
        w_total[:, : 4 * channels],
        s_total[0],
        s_total[3 : 3 + heads].T,
        w_total[:, 4 * channels :],
        s_total[1],
        s_total[2],
    )


def solution(mesh):
    placed = (
        P("dp", "row", None, None),
        P("dp", "row", None, None),
        P("dp"),
        P(),
        P(),
        P(),
        P(),
        P(),
        P(),
    )
    return jax.shard_map(
        body,
        mesh=mesh,
        in_specs=placed,
        out_specs=(P("dp", "row", None, None), P(), P(), P(), P(), P(), P()),
        check_vma=False,
    )
```

time: 965 us -> 290 us (0.30)
  matrix products: 308 us -> 0 us
  waiting for transfers between devices: 257 us -> 44.1 us
  other arithmetic: 141 us -> 6.18 us
  local copies, waits for them, and re-layouts: 152 us -> 34.7 us
  Pallas kernels: 0 us -> 107 us
  between operations: 14.7 us -> 1.44 us
  starting transfers between devices: 17.8 us -> 28.2 us
    dot_general x69 -> x0, matrix products: 308 us -> none  [the longest x6 87.7 us: block_step(): jnp.einsum('ibhd,kbhd->bhki', d_attended, value_blk, preferred_element_ty...]
    psum x1 -> x0, waiting for transfers between devices: 148 us -> none  [body(): lax.psum((proj_grad, gate_grad, bias_w_grad, out_grad, gain_side, shift_s...]
    pallas_call x0 -> x5, Pallas kernels: none -> 107 us  [the longest x2 89.3 us: columns_call(): pl.pallas_call(functools.partial(columns_kernel, heads, first, last, col0...]
    reduce_sum x22 -> x4, other arithmetic: 92.7 us -> 3.96 us  [the longest x1 1.36 us: body(): s_total = jnp.sum(told[:, held:], axis=0) / n]
    psum x1 -> x0, blocking collectives: 68.1 us -> none  [body(): lax.psum((proj_grad, gate_grad, bias_w_grad, out_grad, gain_side, shift_s...]
    all_to_all x0 -> x3, blocking collectives: none -> 66.3 us  [exchange(): return lax.all_to_all(a, axis, 0, 0)]
    unnamed x4 -> x0, waiting for transfers between devices: 51.1 us -> none
    concatenate x24 -> x0, local copies, waits for them, and re-layouts: 46.9 us -> none  [block_step(): jnp.concatenate(pieces, axis=-1).astype(jnp.bfloat16)]
  transfers between devices with their start and end apart: 6 -> 5, of which waited for: 5 -> 4; matrix products, arithmetic and copies ran while one was open for 4% -> 9% of each run, Pallas kernels for 0% -> 20%
where the time goes in v1:
time: 290 us; the launch traced here: 288 us
  Pallas kernels  107 us (37%)
  blocking collectives  66.3 us (23%)
  waiting for transfers between devices  44.1 us (15%)
  local copies, waits for them, and re-layouts  34.7 us (12%)
  starting transfers between devices  28.2 us (10%)
  other arithmetic  6.18 us (2%)
    pallas_call x2, Pallas kernels, columns_call(): pl.pallas_call(functools.partial(columns_kernel, heads, first, last, col0...  89.3 us
    all_to_all x3, blocking collectives, exchange(): return lax.all_to_all(a, axis, 0, 0)  66.3 us
    all_to_all x5, waiting for transfers between devices, exchange(): return lax.all_to_all(a, axis, 0, 0)  44.1 us
    all_to_all x5, starting transfers between devices, exchange(): return lax.all_to_all(a, axis, 0, 0)  28.2 us
    unnamed x29, local copies, waits for them, and re-layouts  16.4 us
    pallas_call x1, Pallas kernels, body(): pl.pallas_call(functools.partial(norm_back_kernel, CHUNKS), grid=(n // ti...  9.25 us
  transfers between devices with their start and end apart: 5, of which 4 were waited for; matrix products, arithmetic and copies ran while one was open for 9% of the time, Pallas kernels for 20%

profile of v1, /device:TPU:1, one launch (start us, length us, event | category | flops | bytes accessed | tf_op | source)
XLA Modules:
  0.0 288.1 jit_solution(17596352022711365021)
XLA Ops:
  1.9 5.3 %shard_map.144 = f32[8,24,384]{2,1,0:T(8,128)} custom-call(bf16[24,384,128]{2,1,0:T(8,128)(2,1)} %bitcast.36, f32[1,128]{1,0:T(1,128)} %bitcast.39, f32[1,128]{1,0:T(1,128)} %bitcast.44, bf16[8,128]{1,0:T(8,128)(2,1)} %scatter.4.wbt_ref), custom_call_target="tpu_custom_call" | custom-call | tf_op jit(solution)/shard_map/pallas_call | solution.py:249
  9.4 7.3 %all-to-all-start.2 = ((bf16[16,4,24,384]{3,2,1,0:T(8,128)(2,1)}), bf16[16,4,24,384]{3,2,1,0:T(8,128)(2,1)S(1)}, u32[]{:S(2)}, u32[]{:S(2)}) async-start(bf16[16,4,24,384]{3,2,1,0:T(8,128)(2,1)} %broadcast_in_dim.6), calls=%async_computation.2 | async-start | bytes 2359296 | tf_op jit(solution)/shard_map/all_to_all | solution.py:246
  16.8 2.1 pad_maximum_fusion
  18.9 3.2 %fusion.2 = (bf16[2,24,16,12,128]{4,3,2,1,0:T(8,128)(2,1)S(1)}, bf16[2,24,16,12,128]{4,3,2,1,0:T(8,128)(2,1)}) fusion(bf16[2,24,16,24,128]{4,3,2,1,0:T(8,128)(2,1)S(1)} %bitcast.48), kind=kLoop, calls=%fused_computation.18 | loop fusion | bytes 9437184 | tf_op jit(solution)/shard_map/slice | solution.py:266
  22.1 4.2 %copy.43 = bf16[2,24,16,12,128]{4,1,3,0,2:T(8,128)(2,1)} copy(bf16[2,24,16,12,128]{4,3,2,1,0:T(8,128)(2,1)S(1)} %get-tuple-element.57) | data formatting | bytes 4718592
  26.3 7.6 %all-to-all-done.2.refs_0_ = bf16[16,4,24,384]{3,2,1,0:T(8,128)(2,1)S(1)} async-done(((bf16[16,4,24,384]{3,2,1,0:T(8,128)(2,1)}), bf16[16,4,24,384]{3,2,1,0:T(8,128)(2,1)S(1)}, u32[]{:S(2)}, u32[]{:S(2)}) %all-to-all-start.2) | async-done | bytes 1179680 | tf_op jit(solution)/shard_map/all_to_all | solution.py:246
  34.9 5.0 %all-to-all-start.1 = ((bf16[16,2,12,24,128]{4,3,2,1,0:T(8,128)(2,1)}), bf16[16,2,12,24,128]{4,3,2,1,0:T(8,128)(2,1)}, u32[]{:S(2)}, u32[]{:S(2)}) async-start(bf16[16,2,12,24,128]{4,3,2,1,0:T(8,128)(2,1)} %bitcast.50), calls=%async_computation.1 | async-start | bytes 4718592 | tf_op jit(solution)/shard_map/all_to_all | solution.py:246
  39.9 6.0 %copy.44 = bf16[2,24,16,12,128]{4,1,3,0,2:T(8,128)(2,1)} copy(bf16[2,24,16,12,128]{4,3,2,1,0:T(8,128)(2,1)} %get-tuple-element.58) | data formatting | bytes 4718592
  46.0 24.4 %all-to-all-done.1.pair_ref.cot_ref = bf16[16,2,12,24,128]{4,3,2,1,0:T(8,128)(2,1)} async-done(((bf16[16,2,12,24,128]{4,3,2,1,0:T(8,128)(2,1)}), bf16[16,2,12,24,128]{4,3,2,1,0:T(8,128)(2,1)}, u32[]{:S(2)}, u32[]{:S(2)}) %all-to-all-start.1) | async-done | bytes 2359328 | tf_op jit(solution)/shard_map/all_to_all | solution.py:246
  70.4 5.8 %all-to-all-start = ((bf16[16,2,12,24,128]{4,3,2,1,0:T(8,128)(2,1)}), bf16[16,2,12,24,128]{4,3,2,1,0:T(8,128)(2,1)}, u32[]{:S(2)}, u32[]{:S(2)}) async-start(bf16[16,2,12,24,128]{4,3,2,1,0:T(8,128)(2,1)} %bitcast.49), calls=%async_computation | async-start | bytes 4718592 | tf_op jit(solution)/shard_map/all_to_all | solution.py:246
  78.3 44.6 %shard_map.145 = (bf16[16,12,24,128]{3,2,1,0:T(8,128)(2,1)}, f32[384,1536]{1,0:T(8,128)}, f32[128,640]{1,0:T(8,128)}, f32[3,8,128]{2,1,0:T(8,128)}, f32[384,1536]{1,0:T(8,128)}) custom-call(s32[1]{0:T(128)S(6)} %copy.46.len_ref, s32[1]{0:T(128)} %bitcast.1.own_ref, bf16[16,2,12,24,128]{4,3,2,1,0:T(8,128)(2,1)} %all-to-all-done.1.pair_ref.cot_ref, ...), custom_call_target="tpu_custom_call" | custom-call | flops 2831155200 | bytes 3538944 | tf_op jit(solution)/shard_map/pallas_call | solution.py:163
  122.9 44.7 %shard_map.146 = (bf16[16,12,24,128]{3,2,1,0:T(8,128)(2,1)}, bf16[16,4,24,384]{3,2,1,0:T(8,128)(2,1)}, f32[128,640]{1,0:T(8,128)}, f32[3,8,128]{2,1,0:T(8,128)}) custom-call(s32[1]{0:T(128)S(6)} %copy.46.len_ref, s32[1]{0:T(128)} %bitcast.1.own_ref, bf16[16,2,12,24,128]{4,3,2,1,0:T(8,128)(2,1)} %all-to-all-done.pair_ref.cot_ref, ...), custom_call_target="tpu_custom_call" | custom-call | flops 2831155200 | bytes 3538944 | tf_op jit(solution)/shard_map/pallas_call | solution.py:163
  169.0 23.8 %all_to_all.40 = f32[128,5,128]{2,1,0:T(8,128)} all-to-all(f32[128,5,128]{2,1,0:T(8,128)S(1)} %copy.33), channel_id=1, replica_groups=mesh['dp'=8,'row'=16] {'dp','row'}, dimensions={0} | all-to-all | bytes 655360 | tf_op jit(solution)/shard_map/all_to_all | solution.py:246
  192.8 22.1 %all_to_all.41.parts_ref = bf16[16,4,24,384]{3,2,1,0:T(8,128)(2,1)} all-to-all(bf16[16,4,24,384]{3,2,1,0:T(8,128)(2,1)} %get-tuple-element.34), channel_id=1, replica_groups=mesh['dp'=8,'row'=16] {'row'}, dimensions={0} | all-to-all | bytes 2359296 | tf_op jit(solution)/shard_map/all_to_all | solution.py:246
  214.9 20.4 %all_to_all.42.refs_0_ = bf16[16,12,24,128]{3,2,1,0:T(8,128)(2,1)S(1)} all-to-all(bf16[16,12,24,128]{3,2,1,0:T(8,128)(2,1)S(1)} %copy-done.7), channel_id=1, replica_groups=mesh['dp'=8,'row'=16] {'row'}, dimensions={0} | all-to-all | bytes 2359296 | tf_op jit(solution)/shard_map/all_to_all | solution.py:246
  235.3 4.5 %all-to-all-start.5 = ((bf16[16,12,24,128]{3,2,1,0:T(8,128)(2,1)}), bf16[16,12,24,128]{3,2,1,0:T(8,128)(2,1)}, u32[]{:S(2)}, u32[]{:S(2)}) async-start(bf16[16,12,24,128]{3,2,1,0:T(8,128)(2,1)} %get-tuple-element.37), calls=%async_computation.5 | async-start | bytes 2359296 | tf_op jit(solution)/shard_map/all_to_all | solution.py:246
  243.5 3.4 %shard_map.147 = (f32[4,24,384]{2,1,0:T(8,128)S(1)}, f32[4,384]{1,0:T(4,128)S(1)}) custom-call(bf16[24,384,128]{2,1,0:T(8,128)(2,1)S(1)} %bitcast.37, bf16[16,4,24,384]{3,2,1,0:T(8,128)(2,1)S(1)} %copy-done.1, f32[1,128]{1,0:T(1,128)S(1)} %bitcast.42, f32[1,128]{1,0:T(1,128)S(1)} %bitcast.47), custom_call_target="tpu_custom_call" | custom-call | tf_op jit(solution)/shard_map/pallas_call | solution.py:282
  248.4 8.7 %all-to-all-done.5.refs_1_ = bf16[16,12,24,128]{3,2,1,0:T(8,128)(2,1)} async-done(((bf16[16,12,24,128]{3,2,1,0:T(8,128)(2,1)}), bf16[16,12,24,128]{3,2,1,0:T(8,128)(2,1)}, u32[]{:S(2)}, u32[]{:S(2)}) %all-to-all-start.5) | async-done | bytes 1179680 | tf_op jit(solution)/shard_map/all_to_all | solution.py:246
  258.1 5.5 %all-to-all-start.7 = ((f32[128,12,128]{2,1,0:T(8,128)}), f32[128,12,128]{2,1,0:T(8,128)}, u32[]{:S(2)}, u32[]{:S(2)}) async-start(f32[128,12,128]{2,1,0:T(8,128)} %broadcast_in_dim.8), calls=%async_computation.7 | async-start | bytes 2097152 | tf_op jit(solution)/shard_map/all_to_all | solution.py:246
  263.6 1.8 reshape.75
  265.5 1.8 copy.45
  267.3 1.9 reshape.76
  270.1 9.3 %shard_map.148 = bf16[24,384,128]{2,1,0:T(8,128)(2,1)} custom-call(bf16[24,384,128]{2,1,0:T(8,128)(2,1)S(1)} %bitcast.38, f32[8,8,1152]{2,1,0:T(8,128)S(1)} %pad.7.sums_ref, f32[1,128]{1,0:T(1,128)S(1)} %bitcast.43, bf16[8,128]{1,0:T(8,128)(2,1)S(1)} %copy-done.3, bf16[16,12,24,128]{3,2,1,0:T(8,128)(2,1)S(1)} %all_to_all.42.refs_0_, ...), custom_call_target="tpu_custom_call" | custom-call | tf_op jit(solution)/shard_map/pallas_call | solution.py:309
  279.4 3.4 %all-to-all-done.7 = f32[128,12,128]{2,1,0:T(8,128)} async-done(((f32[128,12,128]{2,1,0:T(8,128)}), f32[128,12,128]{2,1,0:T(8,128)}, u32[]{:S(2)}, u32[]{:S(2)}) %all-to-all-start.7) | async-done | bytes 786464 | tf_op jit(solution)/shard_map/all_to_all | solution.py:246
  (49 shorter events, 19.8 us)
Async XLA Ops:
  7.2 9.5 %copy-start = (bf16[1,24,384,128]{3,2,1,0:T(8,128)(2,1)S(1)}, bf16[1,24,384,128]{3,2,1,0:T(8,128)(2,1)}, u32[]{:S(2)}) copy-start(bf16[1,24,384,128]{3,2,1,0:T(8,128)(2,1)} %param.11) | copy-start | bytes 7077892
  9.4 24.4 %all-to-all-start.2 = ((bf16[16,4,24,384]{3,2,1,0:T(8,128)(2,1)}), bf16[16,4,24,384]{3,2,1,0:T(8,128)(2,1)S(1)}, u32[]{:S(2)}, u32[]{:S(2)}) async-start(bf16[16,4,24,384]{3,2,1,0:T(8,128)(2,1)} %broadcast_in_dim.6), calls=%async_computation.2 | async-start | bytes 2359296 | tf_op jit(solution)/shard_map/all_to_all | solution.py:246
  33.9 1.0 copy-start.6
  34.9 35.5 %all-to-all-start.1 = ((bf16[16,2,12,24,128]{4,3,2,1,0:T(8,128)(2,1)}), bf16[16,2,12,24,128]{4,3,2,1,0:T(8,128)(2,1)}, u32[]{:S(2)}, u32[]{:S(2)}) async-start(bf16[16,2,12,24,128]{4,3,2,1,0:T(8,128)(2,1)} %bitcast.50), calls=%async_computation.1 | async-start | bytes 4718592 | tf_op jit(solution)/shard_map/all_to_all | solution.py:246
  70.4 6.4 %copy-start.8 = (bf16[128,512]{1,0:T(8,128)(2,1)S(1)}, bf16[128,512]{1,0:T(8,128)(2,1)}, u32[]{:S(2)}) copy-start(bf16[128,512]{1,0:T(8,128)(2,1)} %refs_6_.1) | copy-start | bytes 393220
  70.4 7.2 %copy-start.9 = (bf16[128,128]{1,0:T(8,128)(2,1)S(1)}, bf16[128,128]{1,0:T(8,128)(2,1)}, u32[]{:S(2)}) copy-start(bf16[128,128]{1,0:T(8,128)(2,1)} %param.19) | copy-start | bytes 98308
  70.4 52.5 %all-to-all-start = ((bf16[16,2,12,24,128]{4,3,2,1,0:T(8,128)(2,1)}), bf16[16,2,12,24,128]{4,3,2,1,0:T(8,128)(2,1)}, u32[]{:S(2)}, u32[]{:S(2)}) async-start(bf16[16,2,12,24,128]{4,3,2,1,0:T(8,128)(2,1)} %bitcast.49), calls=%async_computation | async-start | bytes 4718592 | tf_op jit(solution)/shard_map/all_to_all | solution.py:246
  169.0 45.9 %copy-start.7 = (bf16[16,12,24,128]{3,2,1,0:T(8,128)(2,1)S(1)}, bf16[16,12,24,128]{3,2,1,0:T(8,128)(2,1)}, u32[]{:S(2)}) copy-start(bf16[16,12,24,128]{3,2,1,0:T(8,128)(2,1)} %get-tuple-element.36) | copy-start | bytes 3538948
  214.9 27.3 %copy-start.4 = (f32[128]{0:T(128)S(1)}, f32[128]{0:T(128)}, u32[]{:S(2)}) copy-start(f32[128]{0:T(128)} %param.14) | copy-start | bytes 1540
  214.9 27.3 %copy-start.5 = (f32[128]{0:T(128)S(1)}, f32[128]{0:T(128)}, u32[]{:S(2)}) copy-start(f32[128]{0:T(128)} %param.15) | copy-start | bytes 1540
  235.3 21.8 %all-to-all-start.5 = ((bf16[16,12,24,128]{3,2,1,0:T(8,128)(2,1)}), bf16[16,12,24,128]{3,2,1,0:T(8,128)(2,1)}, u32[]{:S(2)}, u32[]{:S(2)}) async-start(bf16[16,12,24,128]{3,2,1,0:T(8,128)(2,1)} %get-tuple-element.37), calls=%async_computation.5 | async-start | bytes 2359296 | tf_op jit(solution)/shard_map/all_to_all | solution.py:246
  242.2 1.3 copy-start.1
  243.5 4.8 %copy-start.10 = (f32[3]{0:T(128)S(1)}, f32[3]{0:T(128)}, u32[]{:S(2)}) copy-start(f32[3]{0:T(128)} %pad.11.clone) | copy-start | bytes 40
  246.9 0.7 copy-start.2
  258.1 12.0 %copy-start.3 = (bf16[8,128]{1,0:T(8,128)(2,1)S(1)}, bf16[8,128]{1,0:T(8,128)(2,1)}, u32[]{:S(2)}) copy-start(bf16[8,128]{1,0:T(8,128)(2,1)} %scatter.4.wbt_ref) | copy-start | bytes 6148
  258.1 24.6 %all-to-all-start.7 = ((f32[128,12,128]{2,1,0:T(8,128)}), f32[128,12,128]{2,1,0:T(8,128)}, u32[]{:S(2)}, u32[]{:S(2)}) async-start(f32[128,12,128]{2,1,0:T(8,128)} %broadcast_in_dim.8), calls=%async_computation.7 | async-start | bytes 2097152 | tf_op jit(solution)/shard_map/all_to_all | solution.py:246

commit v2 on v0

v2 whole, which is shorter than its diff:
```python
import functools
import math

import jax
import jax.numpy as jnp
from jax import lax
from jax.experimental import pallas as pl
from jax.experimental.pallas import tpu as pltpu
from jax.sharding import PartitionSpec as P

F32, BF = jnp.float32, jnp.bfloat16
EPSILON = 1e-05
LOG2E = 1.4426950408889634
LN2 = 0.6931471805599453
NN = (((1,), (0,)), ((), ()))
NT = (((1,), (1,)), ((), ()))
TN = (((0,), (0,)), ((), ()))
MIB = 2**20
DEAD = -1e30
CHUNKS = (12, 12)
SAFE = 1e28


def dot(a, b, dims=NN):
    return lax.dot_general(a, b, dims, preferred_element_type=F32)


def halves(a):
    high = a.astype(BF)
    return jnp.concatenate([high, (a - high.astype(F32)).astype(BF)], axis=1)


def lane_mean(a):
    channels = a.shape[1]
    a = a if a.dtype == BF else halves(a)
    return dot(a, jnp.full((a.shape[1], channels), 1.0 / channels, BF))


def norm_parts(x):
    centered = x.astype(F32) - lane_mean(x)
    scale = lax.rsqrt(lane_mean(centered * centered) + EPSILON)
    return centered * scale, scale


def fold_rows(a):
    return jnp.sum(a.reshape(a.shape[0] // 8, 8, a.shape[1]), axis=0)


def send_kernel(heads, pair_ref, cot_ref, gain_ref, shift_ref, wbt_ref, *refs):
    outs, plane = refs[:-1], refs[-1]
    rows, n, channels = pair_ref.shape
    thirds = n // channels
    step = pl.program_id(0)

    @pl.when(step == 0)
    def _():
        for r in range(rows):
            xhat, _ = norm_parts(pair_ref[r])
            normed = (xhat * gain_ref[...] + shift_ref[...]).astype(BF)
            logits = dot(wbt_ref[...], normed, NT)
            for h in range(heads):
                for t in range(thirds):
                    piece = logits[h : h + 1, t * channels : (t + 1) * channels]
                    plane[h * thirds + t, r : r + 1, :] = piece

    block = outs[0].shape[0]
    width = block * rows
    span = pl.ds(pl.multiple_of(step * width, width), width)
    for s in range(block):
        outs[0][s, : heads * thirds] = plane[...].astype(BF)
    for a, ref in enumerate((pair_ref, cot_ref)):
        cells = jnp.swapaxes(ref[:, span, :].astype(F32), 0, 1).astype(BF)
        for s in range(block):
            start = s * rows
            for c, (out, w) in enumerate(zip(outs, CHUNKS)):
                skip = a * w + (heads * thirds if c == 0 else 0)
                out[s, skip : skip + w] = cells[start : start + w]
                start += w


def columns_kernel(heads, first, last, col0, len_ref, own_ref, cells_ref, *refs):
    if not first:
        (bias_ref, bacc_in, wacc_in, sacc_in), refs = refs[:4], refs[4:]
    gain_ref, shift_ref, wp_ref, wpt_ref, gb_ref, wot_ref = refs[:6]
    refs = refs[6:]
    out_ref, sacc_ref = refs[:2]
    refs = refs[2:]
    if not last:
        (bacc_ref, wacc_ref), refs = refs[:2], refs[2:]
    if first:
        bias_ref, refs = refs[0], refs[1:]
    e_ref, ds_ref, kbd, vaug, off_ref = refs[:5]
    if last:
        bacc_ref, wacc_ref = refs[5:]
    step, cols = pl.program_id(0), pl.num_programs(0)
    n, channels = bacc_ref.shape[0], wp_ref.shape[0]
    size, thirds, src = channels // heads, n // channels, cells_ref.shape[0]
    slots = heads * thirds
    skip_in = slots if first else 0
    skip_out = slots + 5 if last else 0
    lane = lax.broadcasted_iota(jnp.int32, (1, channels), 1)
    masks = [jnp.where(lane // size == h, 1.0, 0.0).astype(BF) for h in range(heads)]
    length = len_ref[0]

    def begin():
        if first:
            bacc_ref[...] = jnp.zeros_like(bacc_ref)
            wacc_ref[...] = jnp.zeros_like(wacc_ref)
            sacc_ref[...] = jnp.zeros_like(sacc_ref)
        else:
            bacc_ref[...] = bacc_in[...]
            wacc_ref[...] = wacc_in[...]
            sacc_ref[...] = sacc_in[...]

    @pl.when(step == 0)
    def _():
        if first:
            kpos = lax.broadcasted_iota(jnp.int32, (1, n), 1)
            for h in range(heads):
                for t in range(thirds):
                    plane = cells_ref[:, h * thirds + t].astype(F32).reshape(n, channels)
                    bias_ref[t * channels : (t + 1) * channels, h * n : (h + 1) * n] = jnp.where(
                        kpos < length, plane.T * LOG2E, DEAD
                    )
        begin()
        off_ref[...] = jnp.zeros_like(off_ref)
        for h in range(heads):
            vaug[h * n : (h + 1) * n, channels:] = jnp.broadcast_to(masks[h], (n, channels))

    def column(j, shifted):
        xhat, _ = norm_parts(cells_ref[:, skip_in + j].astype(F32).reshape(n, channels).astype(BF))
        normed_f = xhat * gain_ref[...] + shift_ref[...]
        proj = dot(normed_f.astype(BF), wp_ref[...])
        q_f = proj[:, :channels] * (LOG2E / math.sqrt(size))
        k = proj[:, channels : 2 * channels].astype(BF)
        v = proj[:, 2 * channels : 3 * channels].astype(BF)
        gate = jax.nn.sigmoid(proj[:, 3 * channels :] + gb_ref[...])
        for h in range(heads):
            kbd[h * n : (h + 1) * n, :] = k * masks[h]
            vaug[h * n : (h + 1) * n, :channels] = v * masks[h]
        live = lax.broadcasted_iota(jnp.int32, (n, 1), 0) < length
        live = live & (own_ref[0] + col0 + j < length)
        cot = cells_ref[:, skip_in + cols + j].astype(F32).reshape(n, channels)
        cot = jnp.where(live, cot, 0.0).astype(BF)
        d_out = dot(cot, wot_ref[...])

        scores = dot(q_f.astype(BF), kbd[...], NT) + bias_ref[...]
        if shifted:
            for h in range(heads):
                part = scores[:, h * n : (h + 1) * n]
                part = jnp.exp2(part - jnp.max(part, axis=1, keepdims=True))
                e_ref[:, h * n : (h + 1) * n] = part.astype(BF)
        else:
            e_ref[...] = jnp.exp2(scores).astype(BF)
        summed = dot(e_ref[...], vaug[...])
        total = summed[:, channels:]
        if not shifted:
            fits = (total > 1.0 / SAFE) & (total < SAFE)
            off_ref[...] += fold_rows(jnp.where(fits, 0.0, 1.0))
        recip = 1.0 / total
        att = summed[:, :channels] * recip
        d_att = d_out * gate
        d_gate = d_att * att * (1.0 - gate)
        d_att_b = (d_att * recip).astype(BF)
        d_att_f = d_att_b.astype(F32)
        gi = lax.broadcasted_iota(jnp.int32, (2 * channels, channels), 0) % channels
        gj = lax.broadcasted_iota(jnp.int32, (2 * channels, channels), 1)
        group = jnp.where((gi // size == gj // size) & (gj % size < 2), -1.0, 0.0).astype(BF)
        row_dot = dot(halves(d_att_f * att), group)
        row_hi = row_dot.astype(BF).astype(F32)
        row_lanes = jnp.where(lane % size == 0, row_hi, row_dot - row_hi).astype(BF)
        d_probs = dot(jnp.concatenate([d_att_b, row_lanes], axis=1), vaug[...], NT)
        ds = e_ref[...].astype(F32) * d_probs
        bacc_ref[...] += ds
        ds_ref[...] = ds.astype(BF)
        d_query = dot(ds_ref[...], kbd[...]) * (1.0 / math.sqrt(size))
        q_t, d_att_t = q_f.T.astype(BF), d_att_f.T.astype(BF)
        dk_t, dv_t = [], []
        for p in range(heads // 2):
            rows = slice(2 * p * size, 2 * (p + 1) * size)
            lanes = slice(2 * p * n, 2 * (p + 1) * n)
            both = dot(q_t[rows], ds_ref[:, lanes])
            dk_t += [both[:size, :n], both[size:, n:]]
            both = dot(d_att_t[rows], e_ref[:, lanes])
            dv_t += [both[:size, :n], both[size:, n:]]
        d_key = (jnp.concatenate(dk_t, axis=0) * LN2).T
        d_value = jnp.concatenate(dv_t, axis=0).T
        d_proj = jnp.concatenate([g.astype(BF) for g in (d_query, d_key, d_value, d_gate)], axis=1)
        dn = dot(d_proj, wpt_ref[...])
        out_ref[:, skip_out + j] = dn.reshape(src, n // src, channels).astype(BF)
        gated = gate * att
        wacc_ref[:, : 4 * channels] += dot(normed_f.T.astype(BF), d_proj)
        wacc_ref[:, 4 * channels :] += dot(gated.T.astype(BF), cot)
        sacc_ref[0] += fold_rows(d_gate)
        sacc_ref[1] += fold_rows(dn * xhat)
        sacc_ref[2] += fold_rows(dn)

    column(step, False)

    @pl.when(step == cols - 1)
    def _():
        @pl.when(jnp.max(off_ref[...]) > 0.0)
        def _():
            begin()

            @pl.loop(0, cols)
            def _(j):
                column(j, True)

        if last:
            for h in range(heads):
                for t in range(thirds):
                    plane = bacc_ref[t * channels : (t + 1) * channels, h * n : (h + 1) * n].T
                    out_ref[:, h * thirds + t] = plane.reshape(src, n // src, channels).astype(BF)
            for w in range(5):
                part = wacc_ref[:, w * channels : (w + 1) * channels].reshape(src, -1, channels)
                terms = []
                for _ in range(3):
                    terms.append(part.astype(BF).astype(F32))
                    part = part - terms[-1]
                out_ref[:, slots + w] = jnp.concatenate(terms, axis=1).astype(BF)


def whole(shape):
    return pl.BlockSpec(shape, lambda j: (0,) * len(shape))


def columns_call(first, last, col0, cols, length, own, moved, state, weights, heads):
    src, _, rows, channels = moved.shape
    n = src * rows
    slots = heads * n // channels
    smem = pl.BlockSpec(memory_space=pltpu.SMEM)
    plane = jax.ShapeDtypeStruct((n, heads * n), F32)
    wide = jax.ShapeDtypeStruct((channels, 5 * channels), F32)
    outs = [
        jax.ShapeDtypeStruct((src, cols + (slots + 5 if last else 0), rows, channels), BF),
        jax.ShapeDtypeStruct((3, 8, channels), F32),
    ]
    outs += ([] if last else [plane, wide]) + ([plane] if first else [])
    inputs = (moved, *state, *weights)
    return pl.pallas_call(
        functools.partial(columns_kernel, heads, first, last, col0),
        grid=(cols,),
        in_specs=[smem, smem] + [whole(a.shape) for a in inputs],
        out_specs=[whole(o.shape) for o in outs],
        out_shape=outs,
        scratch_shapes=[
            pltpu.VMEM((n, heads * n), BF),
            pltpu.VMEM((n, heads * n), BF),
            pltpu.VMEM((heads * n, channels), BF),
            pltpu.VMEM((heads * n, 2 * channels), BF),
            pltpu.VMEM((8, channels), F32),
        ]
        + ([pltpu.VMEM(o.shape, F32) for o in (plane, wide)] if last else []),
        compiler_params=pltpu.CompilerParams(
            vmem_limit_bytes=56 * MIB, dimension_semantics=("arbitrary",)
        ),
        cost_estimate=pl.CostEstimate(
            flops=cols * 4 * 10**9, bytes_accessed=cols * n * channels * 6, transcendentals=0
        ),
    )(length, own, *inputs)


def side_kernel(heads, pair_ref, parts_ref, gain_ref, shift_ref, wbt_ref, sacc_ref, sum_ref, share_ref):
    rows, n, channels = pair_ref.shape
    thirds = n // channels
    slots = heads * thirds
    total = jnp.sum(parts_ref[:, :slots].astype(F32), axis=0).astype(BF).astype(F32)
    for h in range(heads):
        for t in range(thirds):
            sum_ref[h, :, t * channels : (t + 1) * channels] = total[h * thirds + t]
    for w in range(5):
        part = jnp.sum(parts_ref[:, slots + w].astype(F32), axis=0)
        share_ref[w] = part[:8] + part[8:16] + part[16:24]
    stats = jnp.zeros((8, 2 * channels), F32)
    flat = jnp.zeros((heads, n), F32)
    none = jnp.zeros((8 - heads, n), F32)
    for r in range(rows):
        xhat, _ = norm_parts(pair_ref[r])
        normed = (xhat * gain_ref[...] + shift_ref[...]).astype(BF)
        own = sum_ref[:, r, :]
        flat = flat + own
        padded = jnp.concatenate([own, none], axis=0).astype(BF)
        stats = stats + dot(padded, jnp.concatenate([normed, xhat.astype(BF)], axis=1))
    wide = wbt_ref[...].astype(F32)
    share_ref[5, 0:1, :] = jnp.sum(sacc_ref[0], axis=0, keepdims=True)
    gain_part = wide * stats[:, channels:]
    share_ref[5, 1:2, :] = jnp.sum(sacc_ref[1] + gain_part, axis=0, keepdims=True)
    shift_part = wide[:heads] * jnp.sum(flat, axis=1, keepdims=True)
    shift_all = jnp.sum(sacc_ref[2], axis=0, keepdims=True)
    share_ref[5, 2:3, :] = shift_all + jnp.sum(shift_part, axis=0, keepdims=True)
    share_ref[5, 3 : 3 + heads, :] = stats[:heads, :channels]
    share_ref[5, 3 + heads :, :] = jnp.zeros((5 - heads, channels), F32)


def norm_back_kernel(pair_ref, sums_ref, gain_ref, wbt_ref, *refs):
    parts, out_ref, side_ref = refs[:-2], refs[-2], refs[-1]
    rows, cols, channels = pair_ref.shape
    heads, n = sums_ref.shape[0], sums_ref.shape[2]
    step = pl.program_id(0)

    @pl.when(step == 0)
    def _():
        none = jnp.zeros((8 - heads, n), F32)
        for r in range(rows):
            own = jnp.concatenate([sums_ref[:, r, :], none], axis=0)
            side_ref[r] = dot(own.T.astype(BF), wbt_ref[...])

    pieces = []
    for s in range(cols // rows):
        for c, (ref, w) in enumerate(zip(parts, CHUNKS)):
            pieces.append(ref[s, ref.shape[1] - w :].astype(F32))
    main = jnp.swapaxes(jnp.concatenate(pieces, axis=0), 0, 1)
    side = side_ref[:, pl.ds(pl.multiple_of(step * cols, cols), cols), :]
    d_normed = (main + side).astype(BF).astype(F32).reshape(rows * cols, channels)
    cells = pair_ref[...].astype(F32).reshape(rows * cols, channels).astype(BF)
    xhat, scale = norm_parts(cells)
    g = d_normed * gain_ref[...]
    dx = scale * (g - lane_mean(g) - xhat * lane_mean(g * xhat))
    out_ref[...] = dx.reshape(rows, cols, channels).astype(BF)


def final_kernel(heads, told_ref, proj_ref, gate_ref, biasw_ref, outw_ref, gain_ref, shift_ref):
    channels = told_ref.shape[-1]
    scale = 1.0 / (told_ref.shape[0] * 24)
    for w in range(5):
        part = told_ref[:, w].reshape(channels, channels) * scale
        if w < 4:
            proj_ref[:, w * channels : (w + 1) * channels] = part
        else:
            outw_ref[...] = part
    small = jnp.sum(told_ref[:, 5], axis=0) * scale
    gate_ref[...] = small[0:1]
    gain_ref[...] = small[1:2]
    shift_ref[...] = small[2:3]
    biasw_ref[...] = small.T[:, 3 : 3 + heads]


def body(pair_rep, grad_out, crop_len, ln_gain, ln_bias, w_proj, gate_bias, w_bias, w_out):
    pair, cot = pair_rep[0], grad_out[0]
    rows, n, channels = pair.shape
    heads = w_bias.shape[1]
    src = n // rows
    slots = heads * n // channels
    own = (lax.axis_index("row") * rows).astype(jnp.int32).reshape(1)
    gain, shift = ln_gain.reshape(1, -1), ln_bias.reshape(1, -1)
    wbt = jnp.zeros((8, channels), BF).at[:heads].set(w_bias.T)
    weights = (gain, shift, w_proj, w_proj.T, gate_bias.reshape(1, -1), w_out.T)

    def exchange(a, axis="row"):
        return lax.all_to_all(a, axis, 0, 0)

    def tell(a, axis):
        return exchange(jnp.broadcast_to(a[None], (lax.axis_size(axis), *a.shape)), axis)

    block = 2
    tile = block * rows
    counts = [2 * w + (slots if c == 0 else 0) for c, w in enumerate(CHUNKS)]
    sent = pl.pallas_call(
        functools.partial(send_kernel, heads),
        grid=(src // block,),
        in_specs=[whole(a.shape) for a in (pair, cot, gain, shift, wbt)],
        out_specs=[pl.BlockSpec((block, w, rows, channels), lambda j: (j, 0, 0, 0)) for w in counts],
        out_shape=[jax.ShapeDtypeStruct((src, w, rows, channels), BF) for w in counts],
        scratch_shapes=[pltpu.VMEM((slots, rows, channels), F32)],
        compiler_params=pltpu.CompilerParams(vmem_limit_bytes=40 * MIB),
    )(pair, cot, gain, shift, wbt)
    moved = [exchange(a) for a in sent]
    starts = [sum(CHUNKS[:c]) for c in range(len(CHUNKS))]
    state, back = (), []
    for c, (start, width, piece) in enumerate(zip(starts, CHUNKS, moved)):
        first, last = c == 0, c == len(CHUNKS) - 1
        out, sacc, *rest = columns_call(
            first, last, start, width, crop_len, own, piece, state, weights, heads
        )
        if not last:
            plane = rest[2] if first else state[0]
            state = (plane, rest[0], rest[1], sacc)
            if back:
                out, back = lax.optimization_barrier((out, back))
            back.append(exchange(out))
    out, back = lax.optimization_barrier((out, back))
    bundle = exchange(out)
    back.append(bundle)

    sums, share = pl.pallas_call(
        functools.partial(side_kernel, heads),
        grid=(1,),
        in_specs=[
            whole(pair.shape),
            pl.BlockSpec((src, slots + 5, rows, channels), lambda j: (0, 0, 0, 0)),
        ]
        + [whole(a.shape) for a in (gain, shift, wbt, sacc)],
        out_specs=[whole((heads, rows, n)), whole((6, 8, channels))],
        out_shape=[
            jax.ShapeDtypeStruct((heads, rows, n), F32),
            jax.ShapeDtypeStruct((6, 8, channels), F32),
        ],
        compiler_params=pltpu.CompilerParams(vmem_limit_bytes=40 * MIB),
    )(pair, bundle, gain, shift, wbt, sacc)
    share = jnp.sum(tell(share, "dp"), axis=0)
    told = tell(share, "row")

    cells = pl.BlockSpec((rows, tile, channels), lambda j: (0, j, 0))
    pair_grad = pl.pallas_call(
        norm_back_kernel,
        grid=(n // tile,),
        in_specs=[cells] + [whole(a.shape) for a in (sums, gain, wbt)]
        + [pl.BlockSpec((block, *a.shape[1:]), lambda j: (j, 0, 0, 0)) for a in back],
        out_specs=cells,
        out_shape=jax.ShapeDtypeStruct(pair.shape, BF),
        scratch_shapes=[pltpu.VMEM((rows, n, channels), F32)],
        compiler_params=pltpu.CompilerParams(vmem_limit_bytes=40 * MIB),
        cost_estimate=pl.CostEstimate(flops=10**10, bytes_accessed=3 * pair.size, transcendentals=0),
    )(pair, sums, gain, wbt, *back)
    proj, gate, biasw, outw, gain_sum, shift_sum = pl.pallas_call(
        functools.partial(final_kernel, heads),
        out_shape=[
            jax.ShapeDtypeStruct(s, F32)
            for s in (
                w_proj.shape,
                (1, channels),
                w_bias.shape,
                w_out.shape,
                (1, channels),
                (1, channels),
            )
        ],
    )(told)
    return (
        pair_grad[None],
        proj,
        gate.reshape(-1),
        biasw,
        outw,
        gain_sum.reshape(-1),
        shift_sum.reshape(-1),
    )


def solution(mesh):
    placed = (
        P("dp", "row", None, None),
        P("dp", "row", None, None),
        P("dp"),
        P(),
        P(),
        P(),
        P(),
        P(),
        P(),
    )
    return jax.shard_map(
        body,
        mesh=mesh,
        in_specs=placed,
        out_specs=(P("dp", "row", None, None), P(), P(), P(), P(), P(), P()),
        check_vma=False,
    )
```

time: 965 us -> 263 us (0.27)
  matrix products: 308 us -> 0 us
  waiting for transfers between devices: 257 us -> 42.2 us
  other arithmetic: 141 us -> 0.02 us
  local copies, waits for them, and re-layouts: 152 us -> 13.8 us
  Pallas kernels: 0 us -> 121 us
  between operations: 14.7 us -> 1.36 us
  blocking collectives: 68.1 us -> 55.1 us
  starting transfers between devices: 17.8 us -> 28 us
    dot_general x69 -> x0, matrix products: 308 us -> none  [the longest x6 87.7 us: block_step(): jnp.einsum('ibhd,kbhd->bhki', d_attended, value_blk, preferred_element_ty...]
    psum x1 -> x0, waiting for transfers between devices: 148 us -> none  [body(): lax.psum((proj_grad, gate_grad, bias_w_grad, out_grad, gain_side, shift_s...]
    pallas_call x0 -> x6, Pallas kernels: none -> 121 us  [the longest x2 91.9 us: columns_call(): pl.pallas_call(functools.partial(columns_kernel, heads, first, last, col0...]
    reduce_sum x22 -> x1, other arithmetic: 92.7 us -> 0.02 us  [body(): share = jnp.sum(tell(share, 'dp'), axis=0)]
    psum x1 -> x0, blocking collectives: 68.1 us -> none  [body(): lax.psum((proj_grad, gate_grad, bias_w_grad, out_grad, gain_side, shift_s...]
    all_to_all x0 -> x2, blocking collectives: none -> 55.1 us  [exchange(): return lax.all_to_all(a, axis, 0, 0)]
    unnamed x4 -> x0, waiting for transfers between devices: 51.1 us -> none
    concatenate x24 -> x0, local copies, waits for them, and re-layouts: 46.9 us -> none  [block_step(): jnp.concatenate(pieces, axis=-1).astype(jnp.bfloat16)]
  transfers between devices with their start and end apart: 6 -> 4, of which waited for: 5 -> 1; matrix products, arithmetic and copies ran while one was open for 4% -> 1% of each run, Pallas kernels for 0% -> 39%
where the time goes in v2:
time: 263 us; the launch traced here: 262 us
  Pallas kernels  121 us (46%)
  blocking collectives  55.1 us (21%)
  waiting for transfers between devices  42.2 us (16%)
  starting transfers between devices  28 us (11%)
  local copies, waits for them, and re-layouts  13.8 us (5%)
    pallas_call x2, Pallas kernels, columns_call(): pl.pallas_call(functools.partial(columns_kernel, heads, first, last, col0...  91.9 us
    all_to_all x2, blocking collectives, exchange(): return lax.all_to_all(a, axis, 0, 0)  55.1 us
    all_to_all x4, waiting for transfers between devices, exchange(): return lax.all_to_all(a, axis, 0, 0)  42.2 us
    all_to_all x4, starting transfers between devices, exchange(): return lax.all_to_all(a, axis, 0, 0)  28 us
    pallas_call x1, Pallas kernels, body(): pl.pallas_call(functools.partial(send_kernel, heads), grid=(src // block,...  13.7 us
    unnamed x33, local copies, waits for them, and re-layouts  12.3 us
    pallas_call x1, Pallas kernels, body(): pl.pallas_call(norm_back_kernel, grid=(n // tile,), in_specs=[cells] + [w...  9.35 us
  transfers between devices with their start and end apart: 4, of which 1 were waited for; matrix products, arithmetic and copies ran while one was open for 1% of the time, Pallas kernels for 39%

profile of v2, /device:TPU:1, one launch (start us, length us, event | category | flops | bytes accessed | tf_op | source)
XLA Modules:
  0.0 261.7 jit_solution(208677528344458469)
XLA Ops:
  0.6 0.7 scatter.4.wbt_ref
  1.3 1.7 copy-done
  3.0 1.7 copy-done.3
  6.0 13.7 %shard_map.144 = (bf16[16,36,24,128]{3,2,1,0:T(8,128)(2,1)}, bf16[16,24,24,128]{3,2,1,0:T(8,128)(2,1)}) custom-call(bf16[24,384,128]{2,1,0:T(8,128)(2,1)S(1)} %bitcast.13, bf16[24,384,128]{2,1,0:T(8,128)(2,1)S(1)} %bitcast.16, f32[1,128]{1,0:T(1,128)S(1)} %bitcast.23, f32[1,128]{1,0:T(1,128)S(1)} %bitcast.19, bf16[8,128]{1,0:T(8,128)(2,1)S(1)} %scatter.4.wbt_ref), custom_call_target="tpu_custom_call" | custom-call | tf_op jit(solution)/shard_map/pallas_call | solution.py:359
  19.7 7.5 %all-to-all-start.1 = ((bf16[16,36,24,128]{3,2,1,0:T(8,128)(2,1)}), bf16[16,36,24,128]{3,2,1,0:T(8,128)(2,1)}, u32[]{:S(2)}, u32[]{:S(2)}) async-start(bf16[16,36,24,128]{3,2,1,0:T(8,128)(2,1)} %get-tuple-element.39), calls=%async_computation.1 | async-start | bytes 7077888 | tf_op jit(solution)/shard_map/all_to_all | solution.py:351
  27.8 0.7 copy.20
  28.5 0.8 copy.19
  29.3 42.2 %all-to-all-done.1.cells_ref = bf16[16,36,24,128]{3,2,1,0:T(8,128)(2,1)} async-done(((bf16[16,36,24,128]{3,2,1,0:T(8,128)(2,1)}), bf16[16,36,24,128]{3,2,1,0:T(8,128)(2,1)}, u32[]{:S(2)}, u32[]{:S(2)}) %all-to-all-start.1) | async-done | bytes 3538976 | tf_op jit(solution)/shard_map/all_to_all | solution.py:351
  71.5 9.7 %all-to-all-start = ((bf16[16,24,24,128]{3,2,1,0:T(8,128)(2,1)}), bf16[16,24,24,128]{3,2,1,0:T(8,128)(2,1)S(1)}, u32[]{:S(2)}, u32[]{:S(2)}) async-start(bf16[16,24,24,128]{3,2,1,0:T(8,128)(2,1)} %get-tuple-element.38), calls=%async_computation | async-start | bytes 4718592 | tf_op jit(solution)/shard_map/all_to_all | solution.py:351
  81.1 45.8 %shard_map.145 = (bf16[16,12,24,128]{3,2,1,0:T(8,128)(2,1)}, f32[3,8,128]{2,1,0:T(8,128)}, f32[384,1536]{1,0:T(8,128)}, f32[128,640]{1,0:T(8,128)}, f32[384,1536]{1,0:T(8,128)}) custom-call(s32[1]{0:T(128)S(6)} %copy.22.len_ref, s32[1]{0:T(128)} %bitcast.1.own_ref, bf16[16,36,24,128]{3,2,1,0:T(8,128)(2,1)} %all-to-all-done.1.cells_ref, f32[1,128]{1,0:T(1,128)} %bitcast.21, ...), custom_call_target="tpu_custom_call" | custom-call | flops 48000000000 | bytes 3538944 | tf_op jit(solution)/shard_map/pallas_call | solution.py:241
  126.9 5.7 %all-to-all-start.2 = ((bf16[16,12,24,128]{3,2,1,0:T(8,128)(2,1)}), bf16[16,12,24,128]{3,2,1,0:T(8,128)(2,1)S(1)}, u32[]{:S(2)}, u32[]{:S(2)}) async-start(bf16[16,12,24,128]{3,2,1,0:T(8,128)(2,1)} %get-tuple-element.45), calls=%async_computation.2 | async-start | bytes 2359296 | tf_op jit(solution)/shard_map/all_to_all | solution.py:351
  132.7 46.1 %shard_map.146 = (bf16[16,29,24,128]{3,2,1,0:T(8,128)(2,1)}, f32[3,8,128]{2,1,0:T(8,128)}) custom-call(s32[1]{0:T(128)S(6)} %copy.22.len_ref, s32[1]{0:T(128)} %bitcast.1.own_ref, bf16[16,24,24,128]{3,2,1,0:T(8,128)(2,1)} %copy-done.11, f32[384,1536]{1,0:T(8,128)} %get-tuple-element.40.refs_0_, f32[384,1536]{1,0:T(8,128)} %get-tuple-element.41.refs_1_, ...), custom_call_target="tpu_custom_call" | custom-call | flops 48000000000 | bytes 3538944 | tf_op jit(solution)/shard_map/pallas_call | solution.py:241
  178.8 1.0 copy-done.4
  179.8 41.0 %all_to_all.30.parts_ref.refs_1_ = bf16[16,29,24,128]{3,2,1,0:T(8,128)(2,1)S(1)} all-to-all(bf16[16,29,24,128]{3,2,1,0:T(8,128)(2,1)} %get-tuple-element.46), channel_id=1, replica_groups=mesh['dp'=8,'row'=16] {'row'}, dimensions={0} | all-to-all | bytes 5701632 | tf_op jit(solution)/shard_map/all_to_all | solution.py:351
  220.9 4.5 %shard_map.147 = (f32[4,24,384]{2,1,0:T(8,128)S(1)}, f32[6,8,128]{2,1,0:T(8,128)S(1)}) custom-call(bf16[24,384,128]{2,1,0:T(8,128)(2,1)S(1)} %bitcast.14, bf16[16,29,24,128]{3,2,1,0:T(8,128)(2,1)S(1)} %all_to_all.30.parts_ref.refs_1_, f32[1,128]{1,0:T(1,128)S(1)} %bitcast.24, f32[1,128]{1,0:T(1,128)S(1)} %bitcast.20, bf16[8,128]{1,0:T(8,128)(2,1)S(1)} %scatter.4.wbt_ref, ...), custom_call_target="tpu_custom_call" | custom-call | tf_op jit(solution)/shard_map/pallas_call | solution.py:386
  225.4 14.1 %all_to_all.31 = f32[8,6,8,128]{3,2,1,0:T(8,128)S(1)} all-to-all(f32[8,6,8,128]{3,2,1,0:T(8,128)S(1)} %broadcast_in_dim.7), channel_id=1, replica_groups=mesh['dp'=8,'row'=16] {'dp'}, dimensions={0} | all-to-all | bytes 393216 | tf_op jit(solution)/shard_map/all_to_all | solution.py:351
  239.5 0.8 broadcast_in_dim.8
  240.3 5.1 %all-to-all-start.5 = ((f32[16,6,8,128]{3,2,1,0:T(8,128)}), f32[16,6,8,128]{3,2,1,0:T(8,128)S(1)}, u32[]{:S(2)}, u32[]{:S(2)}) async-start(f32[16,6,8,128]{3,2,1,0:T(8,128)} %broadcast_in_dim.8), calls=%async_computation.5 | async-start | bytes 786432 | tf_op jit(solution)/shard_map/all_to_all | solution.py:351
  245.4 1.7 copy-done.2
  247.1 1.3 copy-done.5
  248.3 9.4 %shard_map.148 = bf16[24,384,128]{2,1,0:T(8,128)(2,1)} custom-call(bf16[24,384,128]{2,1,0:T(8,128)(2,1)S(1)} %bitcast.15, f32[4,24,384]{2,1,0:T(8,128)S(1)} %get-tuple-element.48.sums_ref, f32[1,128]{1,0:T(1,128)S(1)} %bitcast.25, bf16[8,128]{1,0:T(8,128)(2,1)S(1)} %scatter.4.wbt_ref, bf16[16,12,24,128]{3,2,1,0:T(8,128)(2,1)S(1)} %copy-done.5, ...), custom_call_target="tpu_custom_call" | custom-call | flops 10000000000 | bytes 3538944 | tf_op jit(solution)/shard_map/pallas_call | solution.py:405
  257.7 0.7 copy-done.12
  258.4 1.8 shard_map.149
  260.3 1.5 copy.21
  (29 shorter events, 1.4 us)
Async XLA Ops:
  1.3 1.7 copy-start
  3.0 1.7 copy-start.3
  4.7 0.7 copy-start.7
  5.3 0.7 copy-start.9
  19.7 8.1 %copy-start.14 = (bf16[128,128]{1,0:T(8,128)(2,1)S(1)}, bf16[128,128]{1,0:T(8,128)(2,1)}, u32[]{:S(2)}) copy-start(bf16[128,128]{1,0:T(8,128)(2,1)} %param.19) | copy-start | bytes 98308
  19.7 8.9 %copy-start.13 = (bf16[128,512]{1,0:T(8,128)(2,1)S(1)}, bf16[128,512]{1,0:T(8,128)(2,1)}, u32[]{:S(2)}) copy-start(bf16[128,512]{1,0:T(8,128)(2,1)} %refs_6_.1) | copy-start | bytes 393220
  19.7 51.8 %all-to-all-start.1 = ((bf16[16,36,24,128]{3,2,1,0:T(8,128)(2,1)}), bf16[16,36,24,128]{3,2,1,0:T(8,128)(2,1)}, u32[]{:S(2)}, u32[]{:S(2)}) async-start(bf16[16,36,24,128]{3,2,1,0:T(8,128)(2,1)} %get-tuple-element.39), calls=%async_computation.1 | async-start | bytes 7077888 | tf_op jit(solution)/shard_map/all_to_all | solution.py:351
  71.5 55.5 %all-to-all-start = ((bf16[16,24,24,128]{3,2,1,0:T(8,128)(2,1)}), bf16[16,24,24,128]{3,2,1,0:T(8,128)(2,1)S(1)}, u32[]{:S(2)}, u32[]{:S(2)}) async-start(bf16[16,24,24,128]{3,2,1,0:T(8,128)(2,1)} %get-tuple-element.38), calls=%async_computation | async-start | bytes 4718592 | tf_op jit(solution)/shard_map/all_to_all | solution.py:351
  126.9 5.7 %copy-start.11 = (bf16[16,24,24,128]{3,2,1,0:T(8,128)(2,1)}, bf16[16,24,24,128]{3,2,1,0:T(8,128)(2,1)S(1)}, u32[]{:S(2)}) copy-start(bf16[16,24,24,128]{3,2,1,0:T(8,128)(2,1)S(1)} %all-to-all-done.cells_ref) | copy-start | bytes 7077892
  126.9 51.8 %all-to-all-start.2 = ((bf16[16,12,24,128]{3,2,1,0:T(8,128)(2,1)}), bf16[16,12,24,128]{3,2,1,0:T(8,128)(2,1)S(1)}, u32[]{:S(2)}, u32[]{:S(2)}) async-start(bf16[16,12,24,128]{3,2,1,0:T(8,128)(2,1)} %get-tuple-element.45), calls=%async_computation.2 | async-start | bytes 2359296 | tf_op jit(solution)/shard_map/all_to_all | solution.py:351
  178.8 1.0 copy-start.4
  179.8 41.0 %copy-start.1 = (bf16[1,24,384,128]{3,2,1,0:T(8,128)(2,1)S(1)}, bf16[1,24,384,128]{3,2,1,0:T(8,128)(2,1)}, u32[]{:S(2)}) copy-start(bf16[1,24,384,128]{3,2,1,0:T(8,128)(2,1)} %param.11) | copy-start | bytes 7077892
  179.8 41.0 %copy-start.6 = (f32[3,8,128]{2,1,0:T(8,128)S(1)}, f32[3,8,128]{2,1,0:T(8,128)}, u32[]{:S(2)}) copy-start(f32[3,8,128]{2,1,0:T(8,128)} %get-tuple-element.47.sacc_ref) | copy-start | bytes 36868
  179.8 41.0 %copy-start.8 = (f32[128]{0:T(128)S(1)}, f32[128]{0:T(128)}, u32[]{:S(2)}) copy-start(f32[128]{0:T(128)} %param.15) | copy-start | bytes 1540
  179.8 41.1 %copy-start.10 = (f32[128]{0:T(128)S(1)}, f32[128]{0:T(128)}, u32[]{:S(2)}) copy-start(f32[128]{0:T(128)} %param.14) | copy-start | bytes 1540
  240.3 17.4 %all-to-all-start.5 = ((f32[16,6,8,128]{3,2,1,0:T(8,128)}), f32[16,6,8,128]{3,2,1,0:T(8,128)S(1)}, u32[]{:S(2)}, u32[]{:S(2)}) async-start(f32[16,6,8,128]{3,2,1,0:T(8,128)} %broadcast_in_dim.8), calls=%async_computation.5 | async-start | bytes 786432 | tf_op jit(solution)/shard_map/all_to_all | solution.py:351
  245.4 1.7 copy-start.2
  247.1 1.3 copy-start.5
  257.7 0.7 copy-start.12

commit v3 on v2

--- a/solution.py
+++ b/solution.py
@@ -17,8 +17,9 @@
 TN = (((0,), (0,)), ((), ()))
 MIB = 2**20
 DEAD = -1e30
-CHUNKS = (12, 12)
+CHUNKS = (6, 9, 9)
 SAFE = 1e28
+PAIR, STAGES, LAG = 3, 6, 2
 
 
 def dot(a, b, dims=NN):
@@ -46,41 +47,38 @@
     return jnp.sum(a.reshape(a.shape[0] // 8, 8, a.shape[1]), axis=0)
 
 
-def send_kernel(heads, pair_ref, cot_ref, gain_ref, shift_ref, wbt_ref, *refs):
-    outs, plane = refs[:-1], refs[-1]
+def logits_kernel(heads, pair_ref, gain_ref, shift_ref, wbt_ref, out_ref):
     rows, n, channels = pair_ref.shape
-    thirds = n // channels
-    step = pl.program_id(0)
-
-    @pl.when(step == 0)
-    def _():
-        for r in range(rows):
-            xhat, _ = norm_parts(pair_ref[r])
-            normed = (xhat * gain_ref[...] + shift_ref[...]).astype(BF)
-            logits = dot(wbt_ref[...], normed, NT)
-            for h in range(heads):
-                for t in range(thirds):
-                    piece = logits[h : h + 1, t * channels : (t + 1) * channels]
-                    plane[h * thirds + t, r : r + 1, :] = piece
-
-    block = outs[0].shape[0]
-    width = block * rows
-    span = pl.ds(pl.multiple_of(step * width, width), width)
-    for s in range(block):
-        outs[0][s, : heads * thirds] = plane[...].astype(BF)
+    xhat, _ = norm_parts(pair_ref[...].astype(F32).reshape(rows * n, channels).astype(BF))
+    normed = (xhat * gain_ref[...] + shift_ref[...]).astype(BF)
+    logits = dot(wbt_ref[...], normed, NT)
+    for r in range(rows):
+        for h in range(heads):
+            for t in range(n // channels):
+                start = r * n + t * channels
+                piece = logits[h : h + 1, start : start + channels]
+                out_ref[h * (n // channels) + t, r : r + 1, :] = piece
+
+
+def send_kernel(start, count, pair_ref, cot_ref, *refs):
+    out = refs[-1]
+    block, rows = out.shape[0], pair_ref.shape[0]
+    skip = out.shape[1] - 2 * count
+    if skip:
+        for s in range(block):
+            out[s, :skip] = refs[0][...].astype(BF)
     for a, ref in enumerate((pair_ref, cot_ref)):
-        cells = jnp.swapaxes(ref[:, span, :].astype(F32), 0, 1).astype(BF)
+        cells = jnp.swapaxes(ref[...].astype(F32), 0, 1)
         for s in range(block):
-            start = s * rows
-            for c, (out, w) in enumerate(zip(outs, CHUNKS)):
-                skip = a * w + (heads * thirds if c == 0 else 0)
-                out[s, skip : skip + w] = cells[start : start + w]
-                start += w
+            first = s * rows + start
+            out[s, skip + a * count : skip + (a + 1) * count] = cells[first : first + count].astype(BF)
 
 
 def columns_kernel(heads, first, last, col0, len_ref, own_ref, cells_ref, *refs):
     if not first:
         (bias_ref, bacc_in, wacc_in, sacc_in), refs = refs[:4], refs[4:]
+    if not first and not last:
+        early_ref, refs = refs[0], refs[1:]
     gain_ref, shift_ref, wp_ref, wpt_ref, gb_ref, wot_ref = refs[:6]
     refs = refs[6:]
     out_ref, sacc_ref = refs[:2]
@@ -89,15 +87,15 @@
         (bacc_ref, wacc_ref), refs = refs[:2], refs[2:]
     if first:
         bias_ref, refs = refs[0], refs[1:]
-    e_ref, ds_ref, kbd, vaug, off_ref = refs[:5]
+    e_all, ds_all, kbd_all, vaug_all, off_ref = refs[:5]
     if last:
         bacc_ref, wacc_ref = refs[5:]
-    step, cols = pl.program_id(0), pl.num_programs(0)
+    step, cols = pl.program_id(0), pl.num_programs(0) * PAIR
     n, channels = bacc_ref.shape[0], wp_ref.shape[0]
     size, thirds, src = channels // heads, n // channels, cells_ref.shape[0]
     slots = heads * thirds
     skip_in = slots if first else 0
-    skip_out = slots + 5 if last else 0
+    skip_out = slots + 5 if last else out_ref.shape[1] - cols
     lane = lax.broadcasted_iota(jnp.int32, (1, channels), 1)
     masks = [jnp.where(lane // size == h, 1.0, 0.0).astype(BF) for h in range(heads)]
     length = len_ref[0]
@@ -123,11 +121,15 @@
                         kpos < length, plane.T * LOG2E, DEAD
                     )
         begin()
+        if not first and not last:
+            out_ref[:, :skip_out] = early_ref[...]
         off_ref[...] = jnp.zeros_like(off_ref)
         for h in range(heads):
-            vaug[h * n : (h + 1) * n, channels:] = jnp.broadcast_to(masks[h], (n, channels))
-
-    def column(j, shifted):
+            for u in range(PAIR):
+                vaug_all[u, h * n : (h + 1) * n, channels:] = jnp.broadcast_to(masks[h], (n, channels))
+
+    def column(j, shifted, slot):
+        e_ref, ds_ref, kbd, vaug = e_all.at[slot], ds_all.at[slot], kbd_all.at[slot], vaug_all.at[slot]
         xhat, _ = norm_parts(cells_ref[:, skip_in + j].astype(F32).reshape(n, channels).astype(BF))
         normed_f = xhat * gain_ref[...] + shift_ref[...]
         proj = dot(normed_f.astype(BF), wp_ref[...])
@@ -144,6 +146,7 @@
         cot = jnp.where(live, cot, 0.0).astype(BF)
         d_out = dot(cot, wot_ref[...])
 
+        yield
         scores = dot(q_f.astype(BF), kbd[...], NT) + bias_ref[...]
         if shifted:
             for h in range(heads):
@@ -152,6 +155,7 @@
                 e_ref[:, h * n : (h + 1) * n] = part.astype(BF)
         else:
             e_ref[...] = jnp.exp2(scores).astype(BF)
+        yield
         summed = dot(e_ref[...], vaug[...])
         total = summed[:, channels:]
         if not shifted:
@@ -169,10 +173,12 @@
         row_dot = dot(halves(d_att_f * att), group)
         row_hi = row_dot.astype(BF).astype(F32)
         row_lanes = jnp.where(lane % size == 0, row_hi, row_dot - row_hi).astype(BF)
+        yield
         d_probs = dot(jnp.concatenate([d_att_b, row_lanes], axis=1), vaug[...], NT)
         ds = e_ref[...].astype(F32) * d_probs
         bacc_ref[...] += ds
         ds_ref[...] = ds.astype(BF)
+        yield
         d_query = dot(ds_ref[...], kbd[...]) * (1.0 / math.sqrt(size))
         q_t, d_att_t = q_f.T.astype(BF), d_att_f.T.astype(BF)
         dk_t, dv_t = [], []
@@ -185,6 +191,7 @@
             dv_t += [both[:size, :n], both[size:, n:]]
         d_key = (jnp.concatenate(dk_t, axis=0) * LN2).T
         d_value = jnp.concatenate(dv_t, axis=0).T
+        yield
         d_proj = jnp.concatenate([g.astype(BF) for g in (d_query, d_key, d_value, d_gate)], axis=1)
         dn = dot(d_proj, wpt_ref[...])
         out_ref[:, skip_out + j] = dn.reshape(src, n // src, channels).astype(BF)
@@ -195,17 +202,24 @@
         sacc_ref[1] += fold_rows(dn * xhat)
         sacc_ref[2] += fold_rows(dn)
 
-    column(step, False)
-
-    @pl.when(step == cols - 1)
+    def run(first_col, shifted):
+        ahead = [column(first_col + u, shifted, u) for u in range(PAIR)]
+        for turn in range(STAGES + LAG * (PAIR - 1)):
+            for u in range(PAIR):
+                if LAG * u <= turn < STAGES + LAG * u:
+                    next(ahead[u], None)
+
+    run(step * PAIR, False)
+
+    @pl.when(step == pl.num_programs(0) - 1)
     def _():
         @pl.when(jnp.max(off_ref[...]) > 0.0)
         def _():
             begin()
 
-            @pl.loop(0, cols)
+            @pl.loop(0, cols // PAIR)
             def _(j):
-                column(j, True)
+                run(j * PAIR, True)
 
         if last:
             for h in range(heads):
@@ -233,22 +247,22 @@
     plane = jax.ShapeDtypeStruct((n, heads * n), F32)
     wide = jax.ShapeDtypeStruct((channels, 5 * channels), F32)
     outs = [
-        jax.ShapeDtypeStruct((src, cols + (slots + 5 if last else 0), rows, channels), BF),
+        jax.ShapeDtypeStruct((src, cols + (slots + 5 if last else col0), rows, channels), BF),
         jax.ShapeDtypeStruct((3, 8, channels), F32),
     ]
     outs += ([] if last else [plane, wide]) + ([plane] if first else [])
     inputs = (moved, *state, *weights)
     return pl.pallas_call(
         functools.partial(columns_kernel, heads, first, last, col0),
-        grid=(cols,),
+        grid=(cols // PAIR,),
         in_specs=[smem, smem] + [whole(a.shape) for a in inputs],
         out_specs=[whole(o.shape) for o in outs],
         out_shape=outs,
         scratch_shapes=[
-            pltpu.VMEM((n, heads * n), BF),
-            pltpu.VMEM((n, heads * n), BF),
-            pltpu.VMEM((heads * n, channels), BF),
-            pltpu.VMEM((heads * n, 2 * channels), BF),
+            pltpu.VMEM((PAIR, n, heads * n), BF),
+            pltpu.VMEM((PAIR, n, heads * n), BF),
+            pltpu.VMEM((PAIR, heads * n, channels), BF),
+            pltpu.VMEM((PAIR, heads * n, 2 * channels), BF),
             pltpu.VMEM((8, channels), F32),
         ]
         + ([pltpu.VMEM(o.shape, F32) for o in (plane, wide)] if last else []),
@@ -308,7 +322,7 @@
 
     pieces = []
     for s in range(cols // rows):
-        for c, (ref, w) in enumerate(zip(parts, CHUNKS)):
+        for ref, w in zip(parts, (sum(CHUNKS[:-1]), CHUNKS[-1])):
             pieces.append(ref[s, ref.shape[1] - w :].astype(F32))
     main = jnp.swapaxes(jnp.concatenate(pieces, axis=0), 0, 1)
     side = side_ref[:, pl.ds(pl.multiple_of(step * cols, cols), cols), :]
@@ -320,9 +334,9 @@
     out_ref[...] = dx.reshape(rows, cols, channels).astype(BF)
 
 
-def final_kernel(heads, told_ref, proj_ref, gate_ref, biasw_ref, outw_ref, gain_ref, shift_ref):
+def final_kernel(heads, size, told_ref, proj_ref, gate_ref, biasw_ref, outw_ref, gain_ref, shift_ref):
     channels = told_ref.shape[-1]
-    scale = 1.0 / (told_ref.shape[0] * 24)
+    scale = 1.0 / size
     for w in range(5):
         part = told_ref[:, w].reshape(channels, channels) * scale
         if w < 4:
@@ -333,7 +347,7 @@
     gate_ref[...] = small[0:1]
     gain_ref[...] = small[1:2]
     shift_ref[...] = small[2:3]
-    biasw_ref[...] = small.T[:, 3 : 3 + heads]
+    biasw_ref[...] = small[3 : 3 + heads]
 
 
 def body(pair_rep, grad_out, crop_len, ln_gain, ln_bias, w_proj, gate_bias, w_bias, w_out):
@@ -355,18 +369,35 @@
 
     block = 2
     tile = block * rows
-    counts = [2 * w + (slots if c == 0 else 0) for c, w in enumerate(CHUNKS)]
-    sent = pl.pallas_call(
-        functools.partial(send_kernel, heads),
-        grid=(src // block,),
-        in_specs=[whole(a.shape) for a in (pair, cot, gain, shift, wbt)],
-        out_specs=[pl.BlockSpec((block, w, rows, channels), lambda j: (j, 0, 0, 0)) for w in counts],
-        out_shape=[jax.ShapeDtypeStruct((src, w, rows, channels), BF) for w in counts],
-        scratch_shapes=[pltpu.VMEM((slots, rows, channels), F32)],
-        compiler_params=pltpu.CompilerParams(vmem_limit_bytes=40 * MIB),
-    )(pair, cot, gain, shift, wbt)
+    group = 8
+    plane = pl.pallas_call(
+        functools.partial(logits_kernel, heads),
+        grid=(rows // group,),
+        in_specs=[pl.BlockSpec((group, n, channels), lambda j: (j, 0, 0))]
+        + [whole(a.shape) for a in (gain, shift, wbt)],
+        out_specs=pl.BlockSpec((slots, group, channels), lambda j: (0, j, 0)),
+        out_shape=jax.ShapeDtypeStruct((slots, rows, channels), F32),
+        compiler_params=pltpu.CompilerParams(vmem_limit_bytes=60 * MIB),
+    )(pair, gain, shift, wbt)
+    cells = pl.BlockSpec((rows, tile, channels), lambda j: (0, j, 0))
+
+    def send(start, count, extra):
+        deep = 2 * count + sum(a.shape[0] for a in extra)
+        return pl.pallas_call(
+            functools.partial(send_kernel, start, count),
+            grid=(src // block,),
+            in_specs=[cells, cells] + [whole(a.shape) for a in extra],
+            out_specs=pl.BlockSpec((block, deep, rows, channels), lambda j: (j, 0, 0, 0)),
+            out_shape=jax.ShapeDtypeStruct((src, deep, rows, channels), BF),
+            compiler_params=pltpu.CompilerParams(vmem_limit_bytes=60 * MIB),
+            cost_estimate=pl.CostEstimate(
+                flops=5 * 10**9, bytes_accessed=3 * pair.size, transcendentals=0
+            ),
+        )(pair, cot, *extra)
+
+    starts = [sum(CHUNKS[:c]) for c in range(len(CHUNKS))]
+    sent = [send(a, w, (plane,) if a == 0 else ()) for a, w in zip(starts, CHUNKS)]
     moved = [exchange(a) for a in sent]
-    starts = [sum(CHUNKS[:c]) for c in range(len(CHUNKS))]
     state, back = (), []
     for c, (start, width, piece) in enumerate(zip(starts, CHUNKS, moved)):
         first, last = c == 0, c == len(CHUNKS) - 1
@@ -376,12 +407,13 @@
         if not last:
             plane = rest[2] if first else state[0]
             state = (plane, rest[0], rest[1], sacc)
-            if back:
-                out, back = lax.optimization_barrier((out, back))
-            back.append(exchange(out))
-    out, back = lax.optimization_barrier((out, back))
+            if c == len(CHUNKS) - 2:
+                early = exchange(out)
+            else:
+                state += (out,)
+    out, early = lax.optimization_barrier((out, early))
     bundle = exchange(out)
-    back.append(bundle)
+    back = (early, bundle)
 
     sums, share = pl.pallas_call(
         functools.partial(side_kernel, heads),
@@ -401,7 +433,6 @@
     share = jnp.sum(tell(share, "dp"), axis=0)
     told = tell(share, "row")
 
-    cells = pl.BlockSpec((rows, tile, channels), lambda j: (0, j, 0))
     pair_grad = pl.pallas_call(
         norm_back_kernel,
         grid=(n // tile,),
@@ -414,13 +445,13 @@
         cost_estimate=pl.CostEstimate(flops=10**10, bytes_accessed=3 * pair.size, transcendentals=0),
     )(pair, sums, gain, wbt, *back)
     proj, gate, biasw, outw, gain_sum, shift_sum = pl.pallas_call(
-        functools.partial(final_kernel, heads),
+        functools.partial(final_kernel, heads, n),
         out_shape=[
             jax.ShapeDtypeStruct(s, F32)
             for s in (
                 w_proj.shape,
                 (1, channels),
-                w_bias.shape,
+                (heads, channels),
                 w_out.shape,
                 (1, channels),
                 (1, channels),
@@ -431,7 +462,7 @@
         pair_grad[None],
         proj,
         gate.reshape(-1),
-        biasw,
+        biasw.T,
         outw,
         gain_sum.reshape(-1),
         shift_sum.reshape(-1),

time: 263 us -> 235 us (0.89)
  waiting for transfers between devices: 42.2 us -> 16.7 us
  local copies, waits for them, and re-layouts: 13.8 us -> 8.45 us
  blocking collectives: 55.1 us -> 51.3 us
    all_to_all x4 -> x5, waiting for transfers between devices: 42.2 us -> 16.7 us  [exchange(): return lax.all_to_all(a, axis, 0, 0)]
    pallas_call x2 -> x5, Pallas kernels: 15.5 us -> 26.6 us  [the longest x3 19.5 us: send(): pl.pallas_call(functools.partial(send_kernel, start, count), grid=(src //...]
    pallas_call x2 -> x3, Pallas kernels: 91.9 us -> 82.9 us  [columns_call(): pl.pallas_call(functools.partial(columns_kernel, heads, first, last, col0...]
    unnamed x33 -> x28, local copies, waits for them, and re-layouts: 12.3 us -> 6.39 us
    all_to_all x2, blocking collectives: 55.1 us -> 51.3 us  [exchange(): return lax.all_to_all(a, axis, 0, 0)]
    all_to_all x4 -> x5, starting transfers between devices: 28 us -> 30.1 us  [exchange(): return lax.all_to_all(a, axis, 0, 0)]
  transfers between devices with their start and end apart: 4 -> 5, of which waited for: 1 -> 2; matrix products, arithmetic and copies ran while one was open for 1% -> 1% of each run, Pallas kernels for 39% -> 45%
where the time goes in v3:
time: 235 us; the launch traced here: 231 us
  Pallas kernels  123 us (52%)
  blocking collectives  51.3 us (22%)
  starting transfers between devices  30.1 us (13%)
  waiting for transfers between devices  16.7 us (7%)
  local copies, waits for them, and re-layouts  8.45 us (4%)
    pallas_call x3, Pallas kernels, columns_call(): pl.pallas_call(functools.partial(columns_kernel, heads, first, last, col0...  82.9 us
    all_to_all x2, blocking collectives, exchange(): return lax.all_to_all(a, axis, 0, 0)  51.3 us
    all_to_all x5, starting transfers between devices, exchange(): return lax.all_to_all(a, axis, 0, 0)  30.1 us
    pallas_call x3, Pallas kernels, send(): pl.pallas_call(functools.partial(send_kernel, start, count), grid=(src //...  19.5 us
    all_to_all x5, waiting for transfers between devices, exchange(): return lax.all_to_all(a, axis, 0, 0)  16.7 us
    pallas_call x1, Pallas kernels, body(): pl.pallas_call(norm_back_kernel, grid=(n // tile,), in_specs=[cells] + [w...  9.2 us
    unnamed x28, local copies, waits for them, and re-layouts  6.39 us
    pallas_call x1, Pallas kernels, body(): pl.pallas_call(functools.partial(logits_kernel, heads), grid=(rows // gro...  5.37 us
  transfers between devices with their start and end apart: 5, of which 2 were waited for; matrix products, arithmetic and copies ran while one was open for 1% of the time, Pallas kernels for 45%

profile of v3, /device:TPU:1, one launch (start us, length us, event | category | flops | bytes accessed | tf_op | source)
XLA Modules:
  0.0 231.2 jit_solution(13366316271048694960)
XLA Ops:
  0.6 1.3 scatter.4.wbt_ref
  1.9 5.4 %shard_map.145.refs_0_ = f32[12,24,128]{2,1,0:T(8,128)} custom-call(bf16[24,384,128]{2,1,0:T(8,128)(2,1)} %bitcast.14, f32[1,128]{1,0:T(1,128)} %bitcast.25, f32[1,128]{1,0:T(1,128)} %bitcast.20, bf16[8,128]{1,0:T(8,128)(2,1)} %scatter.4.wbt_ref), custom_call_target="tpu_custom_call" | custom-call | tf_op jit(solution)/shard_map/pallas_call | solution.py:373
  7.3 6.5 %shard_map.146 = bf16[16,24,24,128]{3,2,1,0:T(8,128)(2,1)} custom-call(bf16[24,384,128]{2,1,0:T(8,128)(2,1)} %bitcast.15, bf16[24,384,128]{2,1,0:T(8,128)(2,1)} %bitcast.38, f32[12,24,128]{2,1,0:T(8,128)} %shard_map.145.refs_0_), custom_call_target="tpu_custom_call" | custom-call | flops 5000000000 | bytes 3538944 | tf_op jit(solution)/shard_map/pallas_call | solution.py:386
  13.8 7.5 %all-to-all-start.1 = ((bf16[16,24,24,128]{3,2,1,0:T(8,128)(2,1)}), bf16[16,24,24,128]{3,2,1,0:T(8,128)(2,1)S(1)}, u32[]{:S(2)}, u32[]{:S(2)}) async-start(bf16[16,24,24,128]{3,2,1,0:T(8,128)(2,1)} %shard_map.146), calls=%async_computation.1 | async-start | bytes 4718592 | tf_op jit(solution)/shard_map/all_to_all | solution.py:365
  23.4 6.5 %shard_map.148 = bf16[16,18,24,128]{3,2,1,0:T(8,128)(2,1)} custom-call(bf16[24,384,128]{2,1,0:T(8,128)(2,1)} %bitcast.16, bf16[24,384,128]{2,1,0:T(8,128)(2,1)} %bitcast.39), custom_call_target="tpu_custom_call" | custom-call | flops 5000000000 | bytes 3538944 | tf_op jit(solution)/shard_map/pallas_call | solution.py:386
  29.9 6.5 %shard_map.144 = bf16[16,18,24,128]{3,2,1,0:T(8,128)(2,1)} custom-call(bf16[24,384,128]{2,1,0:T(8,128)(2,1)} %bitcast.17, bf16[24,384,128]{2,1,0:T(8,128)(2,1)} %bitcast.40), custom_call_target="tpu_custom_call" | custom-call | flops 5000000000 | bytes 3538944 | tf_op jit(solution)/shard_map/pallas_call | solution.py:386
  36.4 15.1 %all-to-all-done.1.cells_ref = bf16[16,24,24,128]{3,2,1,0:T(8,128)(2,1)S(1)} async-done(((bf16[16,24,24,128]{3,2,1,0:T(8,128)(2,1)}), bf16[16,24,24,128]{3,2,1,0:T(8,128)(2,1)S(1)}, u32[]{:S(2)}, u32[]{:S(2)}) %all-to-all-start.1) | async-done | bytes 2359328 | tf_op jit(solution)/shard_map/all_to_all | solution.py:365
  51.5 5.9 %all-to-all-start.2 = ((bf16[16,18,24,128]{3,2,1,0:T(8,128)(2,1)}), bf16[16,18,24,128]{3,2,1,0:T(8,128)(2,1)}, u32[]{:S(2)}, u32[]{:S(2)}) async-start(bf16[16,18,24,128]{3,2,1,0:T(8,128)(2,1)} %shard_map.148), calls=%async_computation.2 | async-start | bytes 3538944 | tf_op jit(solution)/shard_map/all_to_all | solution.py:365
  57.4 22.0 %shard_map.147 = (bf16[16,6,24,128]{3,2,1,0:T(8,128)(2,1)}, f32[3,8,128]{2,1,0:T(8,128)}, f32[384,1536]{1,0:T(8,128)}, f32[128,640]{1,0:T(8,128)}, f32[384,1536]{1,0:T(8,128)}) custom-call(s32[1]{0:T(128)S(6)} %copy.20.len_ref, s32[1]{0:T(128)} %bitcast.1.own_ref, bf16[16,24,24,128]{3,2,1,0:T(8,128)(2,1)} %copy-done.8, f32[1,128]{1,0:T(1,128)} %bitcast.26, ...), custom_call_target="tpu_custom_call" | custom-call | flops 24000000000 | bytes 1769472 | tf_op jit(solution)/shard_map/pallas_call | solution.py:255
  79.3 1.5 all-to-all-done.2.cells_ref
  80.9 5.1 %all-to-all-start = ((bf16[16,18,24,128]{3,2,1,0:T(8,128)(2,1)}), bf16[16,18,24,128]{3,2,1,0:T(8,128)(2,1)S(1)}, u32[]{:S(2)}, u32[]{:S(2)}) async-start(bf16[16,18,24,128]{3,2,1,0:T(8,128)(2,1)} %shard_map.144), calls=%async_computation | async-start | bytes 3538944 | tf_op jit(solution)/shard_map/all_to_all | solution.py:365
  86.0 30.4 %shard_map.149 = (bf16[16,15,24,128]{3,2,1,0:T(8,128)(2,1)}, f32[3,8,128]{2,1,0:T(8,128)}, f32[384,1536]{1,0:T(8,128)}, f32[128,640]{1,0:T(8,128)}) custom-call(s32[1]{0:T(128)S(6)} %copy.20.len_ref, s32[1]{0:T(128)} %bitcast.1.own_ref, bf16[16,18,24,128]{3,2,1,0:T(8,128)(2,1)} %all-to-all-done.2.cells_ref, f32[384,1536]{1,0:T(8,128)} %get-tuple-element.40.refs_0_, ...), custom_call_target="tpu_custom_call" | custom-call | flops 35999997952 | bytes 2654208 | tf_op jit(solution)/shard_map/pallas_call | solution.py:255
  116.3 5.7 %all-to-all-start.3 = ((bf16[16,15,24,128]{3,2,1,0:T(8,128)(2,1)}), bf16[16,15,24,128]{3,2,1,0:T(8,128)(2,1)S(1)}, u32[]{:S(2)}, u32[]{:S(2)}) async-start(bf16[16,15,24,128]{3,2,1,0:T(8,128)(2,1)} %get-tuple-element.49), calls=%async_computation.3 | async-start | bytes 2949120 | tf_op jit(solution)/shard_map/all_to_all | solution.py:365
  122.1 30.5 %shard_map.150 = (bf16[16,26,24,128]{3,2,1,0:T(8,128)(2,1)}, f32[3,8,128]{2,1,0:T(8,128)}) custom-call(s32[1]{0:T(128)S(6)} %copy.20.len_ref, s32[1]{0:T(128)} %bitcast.1.own_ref, bf16[16,18,24,128]{3,2,1,0:T(8,128)(2,1)} %copy-done.9, f32[384,1536]{1,0:T(8,128)} %get-tuple-element.40.refs_0_, f32[384,1536]{1,0:T(8,128)} %get-tuple-element.45.refs_1_, ...), custom_call_target="tpu_custom_call" | custom-call | flops 35999997952 | bytes 2654208 | tf_op jit(solution)/shard_map/pallas_call | solution.py:255
  152.6 1.1 copy-done.2
  153.7 37.4 %all_to_all.35.parts_ref.refs_1_ = bf16[16,26,24,128]{3,2,1,0:T(8,128)(2,1)S(1)} all-to-all(bf16[16,26,24,128]{3,2,1,0:T(8,128)(2,1)} %get-tuple-element.50), channel_id=1, replica_groups=mesh['dp'=8,'row'=16] {'row'}, dimensions={0} | all-to-all | bytes 5111808 | tf_op jit(solution)/shard_map/all_to_all | solution.py:365
  191.2 4.5 %shard_map.151 = (f32[4,24,384]{2,1,0:T(8,128)S(1)}, f32[6,8,128]{2,1,0:T(8,128)S(1)}) custom-call(bf16[24,384,128]{2,1,0:T(8,128)(2,1)S(1)} %bitcast.18, bf16[16,26,24,128]{3,2,1,0:T(8,128)(2,1)S(1)} %all_to_all.35.parts_ref.refs_1_, f32[1,128]{1,0:T(1,128)S(1)} %bitcast.29, f32[1,128]{1,0:T(1,128)S(1)} %bitcast.24, bf16[8,128]{1,0:T(8,128)(2,1)S(1)} %copy-done.4, ...), custom_call_target="tpu_custom_call" | custom-call | tf_op jit(solution)/shard_map/pallas_call | solution.py:418
  195.7 13.9 %all_to_all.36 = f32[8,6,8,128]{3,2,1,0:T(8,128)S(1)} all-to-all(f32[8,6,8,128]{3,2,1,0:T(8,128)S(1)} %broadcast_in_dim.7), channel_id=1, replica_groups=mesh['dp'=8,'row'=16] {'dp'}, dimensions={0} | all-to-all | bytes 393216 | tf_op jit(solution)/shard_map/all_to_all | solution.py:365
  209.6 0.8 broadcast_in_dim.8
  210.4 5.9 %all-to-all-start.6 = ((f32[16,6,8,128]{3,2,1,0:T(8,128)}), f32[16,6,8,128]{3,2,1,0:T(8,128)S(1)}, u32[]{:S(2)}, u32[]{:S(2)}) async-start(f32[16,6,8,128]{3,2,1,0:T(8,128)} %broadcast_in_dim.8), calls=%async_computation.6 | async-start | bytes 786432 | tf_op jit(solution)/shard_map/all_to_all | solution.py:365
  216.3 1.7 copy-done.1
  217.9 1.4 copy-done.3
  219.3 9.2 %shard_map.152 = bf16[24,384,128]{2,1,0:T(8,128)(2,1)} custom-call(bf16[24,384,128]{2,1,0:T(8,128)(2,1)S(1)} %bitcast.19, f32[4,24,384]{2,1,0:T(8,128)S(1)} %get-tuple-element.52.sums_ref, f32[1,128]{1,0:T(1,128)S(1)} %bitcast.30, bf16[8,128]{1,0:T(8,128)(2,1)S(1)} %copy-done.4, bf16[16,15,24,128]{3,2,1,0:T(8,128)(2,1)S(1)} %copy-done.3, ...), custom_call_target="tpu_custom_call" | custom-call | flops 10000000000 | bytes 3538944 | tf_op jit(solution)/shard_map/pallas_call | solution.py:436
  229.3 1.7 shard_map.153
  (30 shorter events, 2.3 us)
Async XLA Ops:
  13.8 7.5 %copy-start.11 = (bf16[128,512]{1,0:T(8,128)(2,1)S(1)}, bf16[128,512]{1,0:T(8,128)(2,1)}, u32[]{:S(2)}) copy-start(bf16[128,512]{1,0:T(8,128)(2,1)} %refs_6_.1) | copy-start | bytes 393220
  13.8 8.2 %copy-start.12 = (bf16[128,128]{1,0:T(8,128)(2,1)S(1)}, bf16[128,128]{1,0:T(8,128)(2,1)}, u32[]{:S(2)}) copy-start(bf16[128,128]{1,0:T(8,128)(2,1)} %param.19) | copy-start | bytes 98308
  13.8 37.7 %all-to-all-start.1 = ((bf16[16,24,24,128]{3,2,1,0:T(8,128)(2,1)}), bf16[16,24,24,128]{3,2,1,0:T(8,128)(2,1)S(1)}, u32[]{:S(2)}, u32[]{:S(2)}) async-start(bf16[16,24,24,128]{3,2,1,0:T(8,128)(2,1)} %shard_map.146), calls=%async_computation.1 | async-start | bytes 4718592 | tf_op jit(solution)/shard_map/all_to_all | solution.py:365
  51.5 5.9 %copy-start.8 = (bf16[16,24,24,128]{3,2,1,0:T(8,128)(2,1)}, bf16[16,24,24,128]{3,2,1,0:T(8,128)(2,1)S(1)}, u32[]{:S(2)}) copy-start(bf16[16,24,24,128]{3,2,1,0:T(8,128)(2,1)S(1)} %all-to-all-done.1.cells_ref) | copy-start | bytes 7077892
  51.5 29.4 %all-to-all-start.2 = ((bf16[16,18,24,128]{3,2,1,0:T(8,128)(2,1)}), bf16[16,18,24,128]{3,2,1,0:T(8,128)(2,1)}, u32[]{:S(2)}, u32[]{:S(2)}) async-start(bf16[16,18,24,128]{3,2,1,0:T(8,128)(2,1)} %shard_map.148), calls=%async_computation.2 | async-start | bytes 3538944 | tf_op jit(solution)/shard_map/all_to_all | solution.py:365
  80.9 35.4 %all-to-all-start = ((bf16[16,18,24,128]{3,2,1,0:T(8,128)(2,1)}), bf16[16,18,24,128]{3,2,1,0:T(8,128)(2,1)S(1)}, u32[]{:S(2)}, u32[]{:S(2)}) async-start(bf16[16,18,24,128]{3,2,1,0:T(8,128)(2,1)} %shard_map.144), calls=%async_computation | async-start | bytes 3538944 | tf_op jit(solution)/shard_map/all_to_all | solution.py:365
  116.3 5.7 %copy-start.9 = (bf16[16,18,24,128]{3,2,1,0:T(8,128)(2,1)}, bf16[16,18,24,128]{3,2,1,0:T(8,128)(2,1)S(1)}, u32[]{:S(2)}) copy-start(bf16[16,18,24,128]{3,2,1,0:T(8,128)(2,1)S(1)} %all-to-all-done.cells_ref) | copy-start | bytes 5308420
  116.3 36.3 %all-to-all-start.3 = ((bf16[16,15,24,128]{3,2,1,0:T(8,128)(2,1)}), bf16[16,15,24,128]{3,2,1,0:T(8,128)(2,1)S(1)}, u32[]{:S(2)}, u32[]{:S(2)}) async-start(bf16[16,15,24,128]{3,2,1,0:T(8,128)(2,1)} %get-tuple-element.49), calls=%async_computation.3 | async-start | bytes 2949120 | tf_op jit(solution)/shard_map/all_to_all | solution.py:365
  152.6 1.1 copy-start.2
  153.7 37.5 %copy-start = (bf16[1,24,384,128]{3,2,1,0:T(8,128)(2,1)S(1)}, bf16[1,24,384,128]{3,2,1,0:T(8,128)(2,1)}, u32[]{:S(2)}) copy-start(bf16[1,24,384,128]{3,2,1,0:T(8,128)(2,1)} %param.11) | copy-start | bytes 7077892
  153.7 37.5 %copy-start.4 = (bf16[8,128]{1,0:T(8,128)(2,1)S(1)}, bf16[8,128]{1,0:T(8,128)(2,1)}, u32[]{:S(2)}) copy-start(bf16[8,128]{1,0:T(8,128)(2,1)} %scatter.4.wbt_ref) | copy-start | bytes 6148
  153.7 37.5 %copy-start.5 = (f32[3,8,128]{2,1,0:T(8,128)S(1)}, f32[3,8,128]{2,1,0:T(8,128)}, u32[]{:S(2)}) copy-start(f32[3,8,128]{2,1,0:T(8,128)} %get-tuple-element.51.sacc_ref) | copy-start | bytes 36868
  153.7 37.5 %copy-start.6 = (f32[128]{0:T(128)S(1)}, f32[128]{0:T(128)}, u32[]{:S(2)}) copy-start(f32[128]{0:T(128)} %param.15) | copy-start | bytes 1540
  153.7 37.5 %copy-start.7 = (f32[128]{0:T(128)S(1)}, f32[128]{0:T(128)}, u32[]{:S(2)}) copy-start(f32[128]{0:T(128)} %param.14) | copy-start | bytes 1540
  210.4 18.2 %all-to-all-start.6 = ((f32[16,6,8,128]{3,2,1,0:T(8,128)}), f32[16,6,8,128]{3,2,1,0:T(8,128)S(1)}, u32[]{:S(2)}, u32[]{:S(2)}) async-start(f32[16,6,8,128]{3,2,1,0:T(8,128)} %broadcast_in_dim.8), calls=%async_computation.6 | async-start | bytes 786432 | tf_op jit(solution)/shard_map/all_to_all | solution.py:365
  216.3 1.7 copy-start.1
  217.9 1.4 copy-start.3
  228.5 0.7 copy-start.10

commit v4 on v3

--- a/solution.py
+++ b/solution.py
@@ -68,10 +68,11 @@
         for s in range(block):
             out[s, :skip] = refs[0][...].astype(BF)
     for a, ref in enumerate((pair_ref, cot_ref)):
-        cells = jnp.swapaxes(ref[...].astype(F32), 0, 1)
+        cells = ref[...].astype(F32)
         for s in range(block):
             first = s * rows + start
-            out[s, skip + a * count : skip + (a + 1) * count] = cells[first : first + count].astype(BF)
+            own = jnp.swapaxes(cells[:, first : first + count], 0, 1)
+            out[s, skip + a * count : skip + (a + 1) * count] = own.astype(BF)
 
 
 def columns_kernel(heads, first, last, col0, len_ref, own_ref, cells_ref, *refs):
@@ -217,9 +218,10 @@
         def _():
             begin()
 
-            @pl.loop(0, cols // PAIR)
+            @pl.loop(0, cols)
             def _(j):
-                run(j * PAIR, True)
+                for _ in column(j, True, 0):
+                    pass
 
         if last:
             for h in range(heads):
@@ -286,29 +288,28 @@
     for w in range(5):
         part = jnp.sum(parts_ref[:, slots + w].astype(F32), axis=0)
         share_ref[w] = part[:8] + part[8:16] + part[16:24]
-    stats = jnp.zeros((8, 2 * channels), F32)
+    stats = jnp.zeros((heads, 2 * channels), F32)
     flat = jnp.zeros((heads, n), F32)
-    none = jnp.zeros((8 - heads, n), F32)
     for r in range(rows):
         xhat, _ = norm_parts(pair_ref[r])
         normed = (xhat * gain_ref[...] + shift_ref[...]).astype(BF)
         own = sum_ref[:, r, :]
         flat = flat + own
-        padded = jnp.concatenate([own, none], axis=0).astype(BF)
-        stats = stats + dot(padded, jnp.concatenate([normed, xhat.astype(BF)], axis=1))
+        stats = stats + dot(own.astype(BF), jnp.concatenate([normed, xhat.astype(BF)], axis=1))
     wide = wbt_ref[...].astype(F32)
     share_ref[5, 0:1, :] = jnp.sum(sacc_ref[0], axis=0, keepdims=True)
     gain_part = wide * stats[:, channels:]
-    share_ref[5, 1:2, :] = jnp.sum(sacc_ref[1] + gain_part, axis=0, keepdims=True)
-    shift_part = wide[:heads] * jnp.sum(flat, axis=1, keepdims=True)
+    gain_all = jnp.sum(sacc_ref[1], axis=0, keepdims=True)
+    share_ref[5, 1:2, :] = gain_all + jnp.sum(gain_part, axis=0, keepdims=True)
+    shift_part = wide * jnp.sum(flat, axis=1, keepdims=True)
     shift_all = jnp.sum(sacc_ref[2], axis=0, keepdims=True)
     share_ref[5, 2:3, :] = shift_all + jnp.sum(shift_part, axis=0, keepdims=True)
-    share_ref[5, 3 : 3 + heads, :] = stats[:heads, :channels]
+    share_ref[5, 3 : 3 + heads, :] = stats[:, :channels]
     share_ref[5, 3 + heads :, :] = jnp.zeros((5 - heads, channels), F32)
 
 
-def norm_back_kernel(pair_ref, sums_ref, gain_ref, wbt_ref, *refs):
-    parts, out_ref, side_ref = refs[:-2], refs[-2], refs[-1]
+def norm_back_kernel(first, pair_ref, sums_ref, gain_ref, wbt_ref, *refs):
+    parts, out_ref, side_ref = refs[:2], refs[-2], refs[-1]
     rows, cols, channels = pair_ref.shape
     heads, n = sums_ref.shape[0], sums_ref.shape[2]
     step = pl.program_id(0)
@@ -316,9 +317,11 @@
     @pl.when(step == 0)
     def _():
         none = jnp.zeros((8 - heads, n), F32)
+        span = side_ref.shape[1]
         for r in range(rows):
-            own = jnp.concatenate([sums_ref[:, r, :], none], axis=0)
-            side_ref[r] = dot(own.T.astype(BF), wbt_ref[...])
+            own = jnp.concatenate([sums_ref[:, r, :], none], axis=0).T
+            own = own[first * cols : first * cols + span, :heads].astype(BF)
+            side_ref[r] = dot(own, wbt_ref[...])
 
     pieces = []
     for s in range(cols // rows):
@@ -358,7 +361,7 @@
     slots = heads * n // channels
     own = (lax.axis_index("row") * rows).astype(jnp.int32).reshape(1)
     gain, shift = ln_gain.reshape(1, -1), ln_bias.reshape(1, -1)
-    wbt = jnp.zeros((8, channels), BF).at[:heads].set(w_bias.T)
+    wbt = w_bias.T
     weights = (gain, shift, w_proj, w_proj.T, gate_bias.reshape(1, -1), w_out.T)
 
     def exchange(a, axis="row"):
@@ -430,20 +433,32 @@
         ],
         compiler_params=pltpu.CompilerParams(vmem_limit_bytes=40 * MIB),
     )(pair, bundle, gain, shift, wbt, sacc)
-    share = jnp.sum(tell(share, "dp"), axis=0)
-    told = tell(share, "row")
-
-    pair_grad = pl.pallas_call(
-        norm_back_kernel,
-        grid=(n // tile,),
-        in_specs=[cells] + [whole(a.shape) for a in (sums, gain, wbt)]
-        + [pl.BlockSpec((block, *a.shape[1:]), lambda j: (j, 0, 0, 0)) for a in back],
-        out_specs=cells,
-        out_shape=jax.ShapeDtypeStruct(pair.shape, BF),
-        scratch_shapes=[pltpu.VMEM((rows, n, channels), F32)],
-        compiler_params=pltpu.CompilerParams(vmem_limit_bytes=40 * MIB),
-        cost_estimate=pl.CostEstimate(flops=10**10, bytes_accessed=3 * pair.size, transcendentals=0),
-    )(pair, sums, gain, wbt, *back)
+    def norm_back(first, steps, *written):
+        place = lambda j: (0, j + first, 0)
+        inputs = (pair, sums, gain, wbt, *back)
+        return pl.pallas_call(
+            functools.partial(norm_back_kernel, first),
+            grid=(steps,),
+            in_specs=[pl.BlockSpec((rows, tile, channels), place)]
+            + [whole(a.shape) for a in (sums, gain, wbt)]
+            + [pl.BlockSpec((block, *a.shape[1:]), lambda j: (j + first, 0, 0, 0)) for a in back]
+            + [pl.BlockSpec(memory_space=pl.ANY)] * len(written),
+            out_specs=pl.BlockSpec((rows, tile, channels), place),
+            out_shape=jax.ShapeDtypeStruct(pair.shape, BF),
+            scratch_shapes=[pltpu.VMEM((rows, steps * tile, channels), F32)],
+            input_output_aliases={len(inputs): 0} if written else {},
+            compiler_params=pltpu.CompilerParams(vmem_limit_bytes=60 * MIB),
+            cost_estimate=pl.CostEstimate(
+                flops=6 * 10**9, bytes_accessed=2 * pair.size, transcendentals=0
+            ),
+        )(*inputs, *written)
+
+    blocks = n // tile
+    share = tell(share, "dp")
+    pair_grad = norm_back(0, blocks // 2)
+    share, pair_grad = lax.optimization_barrier((share, pair_grad))
+    told = tell(jnp.sum(share, axis=0), "row")
+    pair_grad = norm_back(blocks // 2, blocks - blocks // 2, pair_grad)
     proj, gate, biasw, outw, gain_sum, shift_sum = pl.pallas_call(
         functools.partial(final_kernel, heads, n),
         out_shape=[

time: 235 us -> 232 us (0.987)
  blocking collectives: 51.3 us -> 37.8 us
  starting transfers between devices: 30.1 us -> 38.3 us
  local copies, waits for them, and re-layouts: 8.45 us -> 4.43 us
  Pallas kernels: 123 us -> 127 us
  waiting for transfers between devices: 16.7 us -> 19.1 us
    all_to_all x2 -> x1, blocking collectives: 51.3 us -> 37.8 us  [exchange(): return lax.all_to_all(a, axis, 0, 0)]
    all_to_all x5 -> x6, starting transfers between devices: 30.1 us -> 38.3 us  [exchange(): return lax.all_to_all(a, axis, 0, 0)]
    pallas_call x1 -> x2, Pallas kernels: 9.2 us -> 13.4 us  [norm_back(): pl.pallas_call(functools.partial(norm_back_kernel, first), grid=(steps,),...]
    unnamed x28, local copies, waits for them, and re-layouts: 6.39 us -> 2.95 us
    all_to_all x5 -> x6, waiting for transfers between devices: 16.7 us -> 19.1 us  [exchange(): return lax.all_to_all(a, axis, 0, 0)]
  transfers between devices with their start and end apart: 5 -> 6, of which waited for: 2 -> 4; matrix products, arithmetic and copies ran while one was open for 1% -> 1% of each run, Pallas kernels for 45% -> 48%
where the time goes in v4:
time: 232 us; the launch traced here: 228 us
  Pallas kernels  127 us (55%)
  starting transfers between devices  38.3 us (17%)
  blocking collectives  37.8 us (16%)
  waiting for transfers between devices  19.1 us (8%)
  local copies, waits for them, and re-layouts  4.43 us (2%)
    pallas_call x3, Pallas kernels, columns_call(): pl.pallas_call(functools.partial(columns_kernel, heads, first, last, col0...  81.9 us
    all_to_all x6, starting transfers between devices, exchange(): return lax.all_to_all(a, axis, 0, 0)  38.3 us
    all_to_all x1, blocking collectives, exchange(): return lax.all_to_all(a, axis, 0, 0)  37.8 us
    pallas_call x3, Pallas kernels, send(): pl.pallas_call(functools.partial(send_kernel, start, count), grid=(src //...  19.7 us
    all_to_all x6, waiting for transfers between devices, exchange(): return lax.all_to_all(a, axis, 0, 0)  19.1 us
    pallas_call x2, Pallas kernels, norm_back(): pl.pallas_call(functools.partial(norm_back_kernel, first), grid=(steps,),...  13.4 us
    pallas_call x1, Pallas kernels, body(): pl.pallas_call(functools.partial(logits_kernel, heads), grid=(rows // gro...  5.39 us
  transfers between devices with their start and end apart: 6, of which 4 were waited for; matrix products, arithmetic and copies ran while one was open for 1% of the time, Pallas kernels for 48%

profile of v4, /device:TPU:1, one launch (start us, length us, event | category | flops | bytes accessed | tf_op | source)
XLA Modules:
  0.0 228.0 jit_solution(2586054876718544752)
XLA Ops:
  0.6 5.4 %shard_map.145.refs_0_ = f32[12,24,128]{2,1,0:T(8,128)} custom-call(bf16[24,384,128]{2,1,0:T(8,128)(2,1)} %bitcast.14, f32[1,128]{1,0:T(1,128)} %bitcast.30, f32[1,128]{1,0:T(1,128)} %bitcast.25, bf16[4,128]{1,0:T(4,128)(2,1)} %bitcast.21), custom_call_target="tpu_custom_call" | custom-call | tf_op jit(solution)/shard_map/pallas_call | solution.py:376
  6.0 6.5 %shard_map.146 = bf16[16,24,24,128]{3,2,1,0:T(8,128)(2,1)} custom-call(bf16[24,384,128]{2,1,0:T(8,128)(2,1)} %bitcast.15, bf16[24,384,128]{2,1,0:T(8,128)(2,1)} %bitcast.43, f32[12,24,128]{2,1,0:T(8,128)} %shard_map.145.refs_0_), custom_call_target="tpu_custom_call" | custom-call | flops 5000000000 | bytes 3538944 | tf_op jit(solution)/shard_map/pallas_call | solution.py:389
  12.5 7.5 %all-to-all-start.1 = ((bf16[16,24,24,128]{3,2,1,0:T(8,128)(2,1)}), bf16[16,24,24,128]{3,2,1,0:T(8,128)(2,1)S(1)}, u32[]{:S(2)}, u32[]{:S(2)}) async-start(bf16[16,24,24,128]{3,2,1,0:T(8,128)(2,1)} %shard_map.146), calls=%async_computation.1 | async-start | bytes 4718592 | tf_op jit(solution)/shard_map/all_to_all | solution.py:368
  20.0 0.8 copy.17
  22.1 6.6 %shard_map.148 = bf16[16,18,24,128]{3,2,1,0:T(8,128)(2,1)} custom-call(bf16[24,384,128]{2,1,0:T(8,128)(2,1)} %bitcast.16, bf16[24,384,128]{2,1,0:T(8,128)(2,1)} %bitcast.44), custom_call_target="tpu_custom_call" | custom-call | flops 5000000000 | bytes 3538944 | tf_op jit(solution)/shard_map/pallas_call | solution.py:389
  28.8 6.6 %shard_map.144 = bf16[16,18,24,128]{3,2,1,0:T(8,128)(2,1)} custom-call(bf16[24,384,128]{2,1,0:T(8,128)(2,1)} %bitcast.17, bf16[24,384,128]{2,1,0:T(8,128)(2,1)} %bitcast.45), custom_call_target="tpu_custom_call" | custom-call | flops 5000000000 | bytes 3538944 | tf_op jit(solution)/shard_map/pallas_call | solution.py:389
  35.4 14.9 %all-to-all-done.1.cells_ref = bf16[16,24,24,128]{3,2,1,0:T(8,128)(2,1)S(1)} async-done(((bf16[16,24,24,128]{3,2,1,0:T(8,128)(2,1)}), bf16[16,24,24,128]{3,2,1,0:T(8,128)(2,1)S(1)}, u32[]{:S(2)}, u32[]{:S(2)}) %all-to-all-start.1) | async-done | bytes 2359328 | tf_op jit(solution)/shard_map/all_to_all | solution.py:368
  50.2 6.5 %all-to-all-start.2 = ((bf16[16,18,24,128]{3,2,1,0:T(8,128)(2,1)}), bf16[16,18,24,128]{3,2,1,0:T(8,128)(2,1)}, u32[]{:S(2)}, u32[]{:S(2)}) async-start(bf16[16,18,24,128]{3,2,1,0:T(8,128)(2,1)} %shard_map.148), calls=%async_computation.2 | async-start | bytes 3538944 | tf_op jit(solution)/shard_map/all_to_all | solution.py:368
  56.8 21.4 %shard_map.147 = (bf16[16,6,24,128]{3,2,1,0:T(8,128)(2,1)}, f32[3,8,128]{2,1,0:T(8,128)}, f32[384,1536]{1,0:T(8,128)}, f32[128,640]{1,0:T(8,128)}, f32[384,1536]{1,0:T(8,128)}) custom-call(s32[1]{0:T(128)S(6)} %copy.20.len_ref, s32[1]{0:T(128)} %bitcast.1.own_ref, bf16[16,24,24,128]{3,2,1,0:T(8,128)(2,1)} %copy-done.7, f32[1,128]{1,0:T(1,128)} %bitcast.31, ...), custom_call_target="tpu_custom_call" | custom-call | flops 24000000000 | bytes 1769472 | tf_op jit(solution)/shard_map/pallas_call | solution.py:257
  78.2 2.0 all-to-all-done.2.cells_ref
  80.1 5.3 %all-to-all-start = ((bf16[16,18,24,128]{3,2,1,0:T(8,128)(2,1)}), bf16[16,18,24,128]{3,2,1,0:T(8,128)(2,1)S(1)}, u32[]{:S(2)}, u32[]{:S(2)}) async-start(bf16[16,18,24,128]{3,2,1,0:T(8,128)(2,1)} %shard_map.144), calls=%async_computation | async-start | bytes 3538944 | tf_op jit(solution)/shard_map/all_to_all | solution.py:368
  85.5 30.4 %shard_map.149 = (bf16[16,15,24,128]{3,2,1,0:T(8,128)(2,1)}, f32[3,8,128]{2,1,0:T(8,128)}, f32[384,1536]{1,0:T(8,128)}, f32[128,640]{1,0:T(8,128)}) custom-call(s32[1]{0:T(128)S(6)} %copy.20.len_ref, s32[1]{0:T(128)} %bitcast.1.own_ref, bf16[16,18,24,128]{3,2,1,0:T(8,128)(2,1)} %all-to-all-done.2.cells_ref, f32[384,1536]{1,0:T(8,128)} %get-tuple-element.30.refs_0_, ...), custom_call_target="tpu_custom_call" | custom-call | flops 35999997952 | bytes 2654208 | tf_op jit(solution)/shard_map/pallas_call | solution.py:257
  115.9 6.0 %all-to-all-start.3 = ((bf16[16,15,24,128]{3,2,1,0:T(8,128)(2,1)}), bf16[16,15,24,128]{3,2,1,0:T(8,128)(2,1)S(1)}, u32[]{:S(2)}, u32[]{:S(2)}) async-start(bf16[16,15,24,128]{3,2,1,0:T(8,128)(2,1)} %get-tuple-element.39), calls=%async_computation.3 | async-start | bytes 2949120 | tf_op jit(solution)/shard_map/all_to_all | solution.py:368
  121.9 30.2 %shard_map.150 = (bf16[16,26,24,128]{3,2,1,0:T(8,128)(2,1)}, f32[3,8,128]{2,1,0:T(8,128)}) custom-call(s32[1]{0:T(128)S(6)} %copy.20.len_ref, s32[1]{0:T(128)} %bitcast.1.own_ref, bf16[16,18,24,128]{3,2,1,0:T(8,128)(2,1)} %copy-done.8, f32[384,1536]{1,0:T(8,128)} %get-tuple-element.30.refs_0_, f32[384,1536]{1,0:T(8,128)} %get-tuple-element.35.refs_1_, ...), custom_call_target="tpu_custom_call" | custom-call | flops 35999997952 | bytes 2654208 | tf_op jit(solution)/shard_map/pallas_call | solution.py:257
  152.2 37.8 %all_to_all.35.parts_ref.refs_1_ = bf16[16,26,24,128]{3,2,1,0:T(8,128)(2,1)S(1)} all-to-all(bf16[16,26,24,128]{3,2,1,0:T(8,128)(2,1)} %get-tuple-element.40), channel_id=1, replica_groups=mesh['dp'=8,'row'=16] {'row'}, dimensions={0} | all-to-all | bytes 5111808 | tf_op jit(solution)/shard_map/all_to_all | solution.py:368
  190.0 4.5 %shard_map.151 = (f32[4,24,384]{2,1,0:T(8,128)S(1)}, f32[6,8,128]{2,1,0:T(8,128)S(1)}) custom-call(bf16[24,384,128]{2,1,0:T(8,128)(2,1)S(1)} %bitcast.20, bf16[16,26,24,128]{3,2,1,0:T(8,128)(2,1)S(1)} %all_to_all.35.parts_ref.refs_1_, f32[1,128]{1,0:T(1,128)S(1)} %bitcast.36, f32[1,128]{1,0:T(1,128)S(1)} %bitcast.29, bf16[4,128]{1,0:T(4,128)(2,1)S(1)} %bitcast.24, ...), custom_call_target="tpu_custom_call" | custom-call | tf_op jit(solution)/shard_map/pallas_call | solution.py:421
  195.8 7.0 %all-to-all-start.5 = ((f32[8,6,8,128]{3,2,1,0:T(8,128)}), f32[8,6,8,128]{3,2,1,0:T(8,128)S(1)}, u32[]{:S(2)}, u32[]{:S(2)}) async-start(f32[8,6,8,128]{3,2,1,0:T(8,128)} %broadcast_in_dim.6), calls=%async_computation.5 | async-start | bytes 393216 | tf_op jit(solution)/shard_map/all_to_all | solution.py:368
  202.9 6.6 %shard_map.152.refs_2_ = bf16[24,384,128]{2,1,0:T(8,128)(2,1)} custom-call(bf16[24,384,128]{2,1,0:T(8,128)(2,1)} %bitcast.18, f32[4,24,384]{2,1,0:T(8,128)} %copy-done.6, f32[1,128]{1,0:T(1,128)} %bitcast.34, bf16[4,128]{1,0:T(4,128)(2,1)} %bitcast.22, bf16[16,15,24,128]{3,2,1,0:T(8,128)(2,1)} %copy-done.10, bf16[16,26,24,128]{3,2,1,0:T(8,128)(2,1)} %copy-done), custom_call_target="tpu_custom_call" | custom-call | flops 6000000000 | bytes 2359296 | tf_op jit(solution)/shard_map/pallas_call | solution.py:439
  209.9 0.8 broadcast_in_dim.8
  210.7 5.9 %all-to-all-start.6 = ((f32[16,6,8,128]{3,2,1,0:T(8,128)}), f32[16,6,8,128]{3,2,1,0:T(8,128)S(1)}, u32[]{:S(2)}, u32[]{:S(2)}) async-start(f32[16,6,8,128]{3,2,1,0:T(8,128)} %broadcast_in_dim.8), calls=%async_computation.6 | async-start | bytes 786432 | tf_op jit(solution)/shard_map/all_to_all | solution.py:368
  216.6 6.7 %shard_map.153 = bf16[24,384,128]{2,1,0:T(8,128)(2,1)} custom-call(bf16[24,384,128]{2,1,0:T(8,128)(2,1)} %bitcast.19, f32[4,24,384]{2,1,0:T(8,128)} %copy-done.6, f32[1,128]{1,0:T(1,128)} %bitcast.35, bf16[4,128]{1,0:T(4,128)(2,1)} %bitcast.23, bf16[16,15,24,128]{3,2,1,0:T(8,128)(2,1)} %copy-done.10, ...), custom_call_target="tpu_custom_call", output_to_operand_aliasing={{}: (6, {})} | custom-call | flops 6000000000 | bytes 2359296 | tf_op jit(solution)/shard_map/pallas_call | solution.py:439
  223.4 1.9 all-to-all-done.6.told_ref
  225.3 0.7 copy-done.9
  226.0 1.7 shard_map.154
  (31 shorter events, 2.6 us)
Async XLA Ops:
  12.5 7.5 %copy-start.11 = (bf16[128,512]{1,0:T(8,128)(2,1)S(1)}, bf16[128,512]{1,0:T(8,128)(2,1)}, u32[]{:S(2)}) copy-start(bf16[128,512]{1,0:T(8,128)(2,1)} %refs_6_.1) | copy-start | bytes 393220
  12.5 8.2 %copy-start.12 = (bf16[128,128]{1,0:T(8,128)(2,1)S(1)}, bf16[128,128]{1,0:T(8,128)(2,1)}, u32[]{:S(2)}) copy-start(bf16[128,128]{1,0:T(8,128)(2,1)} %param.17) | copy-start | bytes 98308
  12.5 37.7 %all-to-all-start.1 = ((bf16[16,24,24,128]{3,2,1,0:T(8,128)(2,1)}), bf16[16,24,24,128]{3,2,1,0:T(8,128)(2,1)S(1)}, u32[]{:S(2)}, u32[]{:S(2)}) async-start(bf16[16,24,24,128]{3,2,1,0:T(8,128)(2,1)} %shard_map.146), calls=%async_computation.1 | async-start | bytes 4718592 | tf_op jit(solution)/shard_map/all_to_all | solution.py:368
  50.2 6.6 %copy-start.7 = (bf16[16,24,24,128]{3,2,1,0:T(8,128)(2,1)}, bf16[16,24,24,128]{3,2,1,0:T(8,128)(2,1)S(1)}, u32[]{:S(2)}) copy-start(bf16[16,24,24,128]{3,2,1,0:T(8,128)(2,1)S(1)} %all-to-all-done.1.cells_ref) | copy-start | bytes 7077892
  50.2 29.9 %all-to-all-start.2 = ((bf16[16,18,24,128]{3,2,1,0:T(8,128)(2,1)}), bf16[16,18,24,128]{3,2,1,0:T(8,128)(2,1)}, u32[]{:S(2)}, u32[]{:S(2)}) async-start(bf16[16,18,24,128]{3,2,1,0:T(8,128)(2,1)} %shard_map.148), calls=%async_computation.2 | async-start | bytes 3538944 | tf_op jit(solution)/shard_map/all_to_all | solution.py:368
  80.1 35.7 %all-to-all-start = ((bf16[16,18,24,128]{3,2,1,0:T(8,128)(2,1)}), bf16[16,18,24,128]{3,2,1,0:T(8,128)(2,1)S(1)}, u32[]{:S(2)}, u32[]{:S(2)}) async-start(bf16[16,18,24,128]{3,2,1,0:T(8,128)(2,1)} %shard_map.144), calls=%async_computation | async-start | bytes 3538944 | tf_op jit(solution)/shard_map/all_to_all | solution.py:368
  115.9 6.0 %copy-start.8 = (bf16[16,18,24,128]{3,2,1,0:T(8,128)(2,1)}, bf16[16,18,24,128]{3,2,1,0:T(8,128)(2,1)S(1)}, u32[]{:S(2)}) copy-start(bf16[16,18,24,128]{3,2,1,0:T(8,128)(2,1)S(1)} %all-to-all-done.cells_ref) | copy-start | bytes 5308420
  115.9 36.2 %all-to-all-start.3 = ((bf16[16,15,24,128]{3,2,1,0:T(8,128)(2,1)}), bf16[16,15,24,128]{3,2,1,0:T(8,128)(2,1)S(1)}, u32[]{:S(2)}, u32[]{:S(2)}) async-start(bf16[16,15,24,128]{3,2,1,0:T(8,128)(2,1)} %get-tuple-element.39), calls=%async_computation.3 | async-start | bytes 2949120 | tf_op jit(solution)/shard_map/all_to_all | solution.py:368
  152.1 37.9 %copy-start.10 = (bf16[16,15,24,128]{3,2,1,0:T(8,128)(2,1)}, bf16[16,15,24,128]{3,2,1,0:T(8,128)(2,1)S(1)}, u32[]{:S(2)}) copy-start(bf16[16,15,24,128]{3,2,1,0:T(8,128)(2,1)S(1)} %all-to-all-done.3.refs_0_) | copy-start | bytes 4423684
  152.1 37.9 %copy-start.1 = (bf16[1,24,384,128]{3,2,1,0:T(8,128)(2,1)S(1)}, bf16[1,24,384,128]{3,2,1,0:T(8,128)(2,1)}, u32[]{:S(2)}) copy-start(bf16[1,24,384,128]{3,2,1,0:T(8,128)(2,1)} %param.9) | copy-start | bytes 7077892
  152.1 37.9 %copy-start.2 = (f32[3,8,128]{2,1,0:T(8,128)S(1)}, f32[3,8,128]{2,1,0:T(8,128)}, u32[]{:S(2)}) copy-start(f32[3,8,128]{2,1,0:T(8,128)} %get-tuple-element.41.sacc_ref) | copy-start | bytes 36868
  152.1 37.9 %copy-start.3 = (bf16[128,4]{0,1:T(4,128)(2,1)S(1)}, bf16[128,4]{0,1:T(4,128)(2,1)}, u32[]{:S(2)}) copy-start(bf16[128,4]{0,1:T(4,128)(2,1)} %param.16) | copy-start | bytes 3076
  152.1 37.9 %copy-start.4 = (f32[128]{0:T(128)S(1)}, f32[128]{0:T(128)}, u32[]{:S(2)}) copy-start(f32[128]{0:T(128)} %param.13) | copy-start | bytes 1540
  152.1 37.9 %copy-start.5 = (f32[128]{0:T(128)S(1)}, f32[128]{0:T(128)}, u32[]{:S(2)}) copy-start(f32[128]{0:T(128)} %param.12) | copy-start | bytes 1540
  190.0 4.5 %copy-start = (bf16[16,26,24,128]{3,2,1,0:T(8,128)(2,1)}, bf16[16,26,24,128]{3,2,1,0:T(8,128)(2,1)S(1)}, u32[]{:S(2)}) copy-start(bf16[16,26,24,128]{3,2,1,0:T(8,128)(2,1)S(1)} %all_to_all.35.parts_ref.refs_1_) | copy-start | bytes 7667716
  194.5 0.7 copy-start.6
  195.8 14.1 %all-to-all-start.5 = ((f32[8,6,8,128]{3,2,1,0:T(8,128)}), f32[8,6,8,128]{3,2,1,0:T(8,128)S(1)}, u32[]{:S(2)}, u32[]{:S(2)}) async-start(f32[8,6,8,128]{3,2,1,0:T(8,128)} %broadcast_in_dim.6), calls=%async_computation.5 | async-start | bytes 393216 | tf_op jit(solution)/shard_map/all_to_all | solution.py:368
  210.7 14.6 %all-to-all-start.6 = ((f32[16,6,8,128]{3,2,1,0:T(8,128)}), f32[16,6,8,128]{3,2,1,0:T(8,128)S(1)}, u32[]{:S(2)}, u32[]{:S(2)}) async-start(f32[16,6,8,128]{3,2,1,0:T(8,128)} %broadcast_in_dim.8), calls=%async_computation.6 | async-start | bytes 786432 | tf_op jit(solution)/shard_map/all_to_all | solution.py:368
  225.3 0.7 copy-start.9
